TPU v7x, 256 devices: a whole 4x4x8 slice. The times are simulated.
256 devices in a mesh: firm: 32 (over x_lo, z, core), day: 8 (over x_hi, y).
Axes of the slice: x: 4 (x_hi: 2, x_lo: 2; x = x_hi * 2 + x_lo), y: 4, z: 8, core: 2. Of those that a mesh axis runs over, the one named last changes fastest.
Arguments:
- residuals: float32 [32768, 16384], P('firm', 'day'), may hold values from -6 to 6
- loadings: float32 [32768, 8], P('firm'), may hold values from -6 to 6
- factor_path: float32 [16384, 8], P('day'), may hold values from -0.18 to 0.18
- start_guess: float32 [16384, 8], P('day'), may hold values from -6 to 6
- cluster_ids: int32 [32768], P('firm'), may hold values from 0 to 511
- sign_bits: int32 [512, 16], replicated, may hold values from 0 to 1
Outputs:
- boot_loadings: float32 [32768, 128], P('firm')
- boot_factors: float32 [16384, 128], P('day')
All inputs are finite; a program needn't handle non-finite values.
Results may differ from a plain program's by a relative error of at most 0.0011.
Values sent between devices are 32-bit elements; how exact they have to be, the bound alone decides.
No kernel may reach another device: no remote copies, remote signals or barrier semaphores. Data moves between devices by JAX's collectives and lax.ppermute only.
A program may use at most 64 MiB of HBM per device.

v0:
```python
import math

import jax
import jax.numpy as jnp
from jax import lax
from jax.sharding import PartitionSpec as P

ITERS = 2


def on_device(residuals, loadings, factor_path, start_guess, cluster_ids, sign_bits):
    highest = lax.Precision.HIGHEST
    reps = sign_bits.shape[1]
    factors = start_guess.shape[1]
    clusters = sign_bits.shape[0]

    def gram_of(matrix):
        blocks = matrix.reshape(matrix.shape[0], reps, factors)
        return jnp.einsum("nbr,nbs->brs", blocks, blocks, precision=highest)

    def inverse_factor(gram_sum):
        lower = jnp.linalg.cholesky(gram_sum)
        eye_blocks = jnp.broadcast_to(jnp.eye(factors, dtype=gram_sum.dtype), lower.shape)
        return lax.linalg.triangular_solve(lower, eye_blocks, left_side=True, lower=True)

    def rotate(matrix, inverse):
        blocks = matrix.reshape(matrix.shape[0], reps, factors)
        return jnp.einsum("nbr,bsr->nbs", blocks, inverse, precision=highest).reshape(matrix.shape)

    def normalize_days(raw_factors):
        gram_sum = lax.psum(gram_of(raw_factors), "day")
        return rotate(raw_factors, inverse_factor(gram_sum))

    member = (cluster_ids[:, None] == jnp.arange(clusters, dtype=jnp.int32)[None, :]).astype(
        residuals.dtype
    )
    table = 2.0 * sign_bits.astype(residuals.dtype) - 1.0
    row_signs = jnp.dot(member, table, precision=highest)
    weights_wide = jnp.repeat(row_signs, factors, axis=1)
    current = jnp.tile(start_guess, (1, reps))
    loads_now = None
    for sweep in range(ITERS):
        day_part = weights_wide * jnp.dot(residuals, current, precision=highest) + jnp.dot(
            loadings, jnp.dot(factor_path.T, current, precision=highest), precision=highest
        )
        raw_loads = lax.psum(day_part, "day")
        normalize_gram_sum = lax.psum(gram_of(raw_loads), "firm")
        loads_now = rotate(raw_loads, inverse_factor(normalize_gram_sum))
        product = lax.dot_general(
            residuals, weights_wide * loads_now, (((0,), (0,)), ((), ())), precision=highest
        )
        raw_factors = lax.psum(
            product
            + jnp.dot(
                factor_path, jnp.dot(loadings.T, loads_now, precision=highest), precision=highest
            ),
            "firm",
        )
        current = normalize_days(raw_factors)
    firm_count = residuals.shape[0] * lax.axis_size("firm")
    day_count = residuals.shape[1] * lax.axis_size("day")
    return (math.sqrt(firm_count) * loads_now, math.sqrt(day_count) * current)


def solution(mesh):
    placed = (P("firm", "day"), P("firm", None), P("day", None), P("day", None), P("firm"), P())
    return jax.shard_map(
        on_device,
        mesh=mesh,
        in_specs=placed,
        out_specs=(P("firm", None), P("day", None)),
        check_vma=False,
    )
```

profile of v0, /device:TPU:1, one launch (start us, length us, event | category | flops | bytes accessed | tf_op | source)
XLA Modules:
  0.0 1072.3 jit_solution(13982164511942232748)
XLA Ops:
  11.6 11.3 %bitcast_multiply_fusion.3 = f32[1024,128]{0,1:T(8,128)S(1)} fusion(f32[1024,2048]{1,0:T(8,128)} %param.9, f32[2048,8]{0,1:T(8,128)} %param.12, f32[1024,16]{0,1:T(8,128)S(1)} %fusion.3), kind=kOutput, calls=%fused_computation.16 | convolution fusion | flops 3221356544 | bytes 9043968 | tf_op jit(solution)/shard_map/dot_general | solution.py:43
  24.5 88.8 %all-reduce.5.cloned.1.call-done = f32[1024,16,8]{0,2,1:T(8,128)} async-done(((f32[1024,16,8]{0,2,1:T(8,128)}), f32[1024,16,8]{0,2,1:T(8,128)}) %all-reduce.5.cloned.1.call-update) | async-done | bytes 524304 | tf_op jit(solution)/shard_map/psum | solution.py:46
  113.4 2.3 fusion.45
  115.7 106.1 %psum.57 = f32[16,8,8]{1,2,0:T(8,128)S(1)} all-reduce(f32[16,8,8]{1,2,0:T(8,128)S(1)} %fusion.45), channel_id=1, replica_groups=mesh['firm'=32,'day'=8] {'firm'}, use_global_device_ids=true, to_apply=%region_1.0 | all-reduce | flops 1024 | bytes 8192 | tf_op jit(solution)/shard_map/psum | solution.py:47
  221.9 11.7 %custom-call.12 = f32[16,8,8]{2,1,0:T(8,128)S(1)} custom-call(f32[16,8,8]{2,1,0:T(8,128)S(1)} %fusion.32), custom_call_target="Cholesky" | custom-call | tf_op jit(solution)/shard_map/jit(cholesky)/cholesky | solution.py:22
  233.9 10.0 custom-call.13
  246.4 7.1 fusion.15
  255.7 221.2 %all-reduce.7.cloned.1.call-done = f32[2048,16,8]{0,2,1:T(8,128)} async-done(((f32[2048,16,8]{0,2,1:T(8,128)}), f32[2048,16,8]{0,2,1:T(8,128)}) %all-reduce.7.cloned.1.call-update) | async-done | bytes 1048592 | tf_op jit(solution)/shard_map/psum | solution.py:52
  476.9 3.7 fusion.47
  480.6 34.6 %psum.59 = f32[16,8,8]{1,2,0:T(8,128)S(1)} all-reduce(f32[16,8,8]{1,2,0:T(8,128)S(1)} %fusion.47), channel_id=1, replica_groups=mesh['firm'=32,'day'=8] {'day'}, use_global_device_ids=true, to_apply=%region_5.8 | all-reduce | flops 1024 | bytes 8192 | tf_op jit(solution)/shard_map/psum | solution.py:31
  515.3 11.7 %custom-call.14 = f32[16,8,8]{2,1,0:T(8,128)S(1)} custom-call(f32[16,8,8]{2,1,0:T(8,128)S(1)} %fusion.29), custom_call_target="Cholesky" | custom-call | tf_op jit(solution)/shard_map/jit(cholesky)/cholesky | solution.py:22
  527.3 10.0 custom-call.15
  540.8 11.2 %bitcast_multiply_fusion.1 = f32[1024,128]{0,1:T(8,128)S(1)} fusion(f32[2048,128]{0,1:T(8,128)S(1)} %convolution_bitcast_fusion, f32[1024,2048]{1,0:T(8,128)} %param.9, f32[1024,16]{0,1:T(8,128)S(1)} %fusion.3), kind=kOutput, calls=%fused_computation.14 | convolution fusion | flops 3221356544 | bytes 10027008 | tf_op jit(solution)/shard_map/dot_general | solution.py:43
  553.5 84.2 %all-reduce.9.cloned.1.call-done = f32[1024,16,8]{0,2,1:T(8,128)} async-done(((f32[1024,16,8]{0,2,1:T(8,128)}), f32[1024,16,8]{0,2,1:T(8,128)}) %all-reduce.9.cloned.1.call-update) | async-done | bytes 524304 | tf_op jit(solution)/shard_map/psum | solution.py:46
  637.8 2.3 fusion.49
  640.0 106.3 %psum.61 = f32[16,8,8]{1,2,0:T(8,128)S(1)} all-reduce(f32[16,8,8]{1,2,0:T(8,128)S(1)} %fusion.49), channel_id=1, replica_groups=mesh['firm'=32,'day'=8] {'firm'}, use_global_device_ids=true, to_apply=%region_7.10 | all-reduce | flops 1024 | bytes 8192 | tf_op jit(solution)/shard_map/psum | solution.py:47
  746.5 11.7 %custom-call.16 = f32[16,8,8]{2,1,0:T(8,128)S(1)} custom-call(f32[16,8,8]{2,1,0:T(8,128)S(1)} %fusion.26), custom_call_target="Cholesky" | custom-call | tf_op jit(solution)/shard_map/jit(cholesky)/cholesky | solution.py:22
  758.4 10.0 custom-call.17
  771.0 7.1 fusion.16
  781.1 220.4 %all-reduce.11.cloned.1.call-done = f32[2048,16,8]{0,2,1:T(8,128)} async-done(((f32[2048,16,8]{0,2,1:T(8,128)}), f32[2048,16,8]{0,2,1:T(8,128)}) %all-reduce.11.cloned.1.call-update) | async-done | bytes 1048592 | tf_op jit(solution)/shard_map/psum | solution.py:52
  1001.5 3.7 fusion.51
  1005.2 34.6 %psum.63 = f32[16,8,8]{1,2,0:T(8,128)S(1)} all-reduce(f32[16,8,8]{1,2,0:T(8,128)S(1)} %fusion.51), channel_id=1, replica_groups=mesh['firm'=32,'day'=8] {'day'}, use_global_device_ids=true, to_apply=%region_9.12 | all-reduce | flops 1024 | bytes 8192 | tf_op jit(solution)/shard_map/psum | solution.py:31
  1039.9 11.7 %custom-call.18 = f32[16,8,8]{2,1,0:T(8,128)S(1)} custom-call(f32[16,8,8]{2,1,0:T(8,128)S(1)} %fusion.23), custom_call_target="Cholesky" | custom-call | tf_op jit(solution)/shard_map/jit(cholesky)/cholesky | solution.py:22
  1051.9 10.0 custom-call.19
  (58 shorter events, 26.5 us)
Async XLA Ops:
  7.2 0.8 copy-start
  7.2 15.8 %copy-start.1 = (f32[1024,8]{0,1:T(8,128)S(1)}, f32[1024,8]{0,1:T(8,128)}, u32[]{:S(2)}) copy-start(f32[1024,8]{0,1:T(8,128)} %param.10) | copy-start | bytes 98308
  7.2 106.2 %all-reduce.5.cloned.1.call-start = ((), (), s32[]{:S(2)}) async-start(), calls=%async_computation | async-start | bytes 1048576 | tf_op jit(solution)/shard_map/psum | solution.py:46
  24.4 452.5 %all-reduce.7.cloned.1.call-start = ((), (), s32[]{:S(2)}) async-start(), calls=%async_computation.1 | async-start | bytes 2097152 | tf_op jit(solution)/shard_map/psum | solution.py:52
  255.5 382.3 %all-reduce.9.cloned.1.call-start = ((), (), s32[]{:S(2)}) async-start(), calls=%async_computation.2 | async-start | bytes 1048576 | tf_op jit(solution)/shard_map/psum | solution.py:46
  553.5 448.0 %all-reduce.11.cloned.1.call-start = ((), (), s32[]{:S(2)}) async-start(), calls=%async_computation.3 | async-start | bytes 2097152 | tf_op jit(solution)/shard_map/psum | solution.py:52
Sparse Core Ops, SparseCore 0:
  24.6 88.7 all-reduce.4
  255.6 221.2 all-reduce.6
  553.6 84.1 all-reduce.8
  780.2 221.2 all-reduce.10
where the time goes:
time: 1080 us; the launch traced here: 1070 us
  waiting for transfers between devices  615 us (57%)
  blocking collectives  282 us (26%)
  other arithmetic  87.7 us (8%)
  matrix products  70.2 us (6%)
  between operations  14 us (1%)
    psum x2, waiting for transfers between devices, on_device(): lax.psum(product + jnp.dot(factor_path, jnp.dot(loadings.T, loads_now, pr...  442 us
    psum x2, blocking collectives, on_device(): normalize_gram_sum = lax.psum(gram_of(raw_loads), 'firm')  212 us
    psum x2, waiting for transfers between devices, on_device(): raw_loads = lax.psum(day_part, 'day')  173 us
    psum x2, blocking collectives, normalize_days(): gram_sum = lax.psum(gram_of(raw_factors), 'day')  69.2 us
    another operation x13, other arithmetic, inverse_factor(): lower = jnp.linalg.cholesky(gram_sum)  47.3 us
    another operation x9, other arithmetic, inverse_factor(): lax.linalg.triangular_solve(lower, eye_blocks, left_side=True, lower=True)  40.4 us
    dot_general x2, matrix products, on_device(): jnp.dot(residuals, current, precision=highest)  22.6 us
  transfers between devices with their start and end apart: 4, of which 4 were waited for; matrix products, arithmetic and copies ran while one was open for 0% of the time, Pallas kernels for 0%

commit v1 on v0

v1 whole, which is shorter than its diff:
```python
import functools
import math

import jax
import jax.numpy as jnp
from jax import lax
from jax.experimental import pallas as pl
from jax.experimental.pallas import tpu as pltpu
from jax.sharding import Mesh
from jax.sharding import PartitionSpec as P

STEPS = 4
HIGHEST = lax.Precision.HIGHEST
NN = (((1,), (0,)), ((), ()))
NT = (((1,), (1,)), ((), ()))
TN = (((0,), (0,)), ((), ()))
PARAMS = pltpu.CompilerParams(vmem_limit_bytes=48 * 1024 * 1024)


def exact(a, b, dims):
    return lax.dot_general(a, b, dims, precision=HIGHEST, preferred_element_type=jnp.float32)


def fast(a, b, dims):
    return lax.dot_general(a, b, dims, preferred_element_type=jnp.float32)


def split(x):
    high = x.astype(jnp.bfloat16)
    return high, (x - high.astype(jnp.float32)).astype(jnp.bfloat16)


def compact(full, factors):
    n = full.shape[0]
    row = lax.broadcasted_iota(jnp.int32, (n, n), 0) // factors
    lane = lax.broadcasted_iota(jnp.int32, (n, n), 1) // factors
    kept = jnp.where(row == lane, full, 0.0)
    return kept.reshape(n // factors, factors, n).sum(axis=0)


def inverse_blocks(gram, factors):
    n = gram.shape[1]
    row = lax.broadcasted_iota(jnp.int32, (factors, n), 0)
    lane = lax.broadcasted_iota(jnp.int32, (factors, n), 1)
    first = (lane // factors) * factors
    rest = gram
    inverse = jnp.where(row == lane - first, 1.0, 0.0)
    for j in range(factors):
        column = jnp.take_along_axis(rest, first + j, axis=1, mode="promise_in_bounds")
        pivot = column[j : j + 1]
        ratio = jnp.where(row > j, column / pivot, 0.0)
        rest = rest - ratio * rest[j : j + 1]
        inverse = inverse - ratio * inverse[j : j + 1]
        inverse = jnp.where(row == j, inverse / jnp.sqrt(pivot), inverse)
    wide = jnp.concatenate([inverse] * (n // factors), axis=0)
    row = lax.broadcasted_iota(jnp.int32, (n, n), 0) // factors
    lane = lax.broadcasted_iota(jnp.int32, (n, n), 1) // factors
    return jnp.where(row == lane, wide, 0.0)


def signs_kernel(ids_ref, bits_ref, wide_ref, tall_ref, *, factors):
    reps, clusters = bits_ref.shape
    firms = ids_ref.shape[1]
    table = 2.0 * bits_ref[...].astype(jnp.float32) - 1.0
    table = jnp.broadcast_to(table[:, None, :], (reps, factors, clusters))
    table = table.reshape(reps * factors, clusters).astype(jnp.bfloat16)
    cluster = lax.broadcasted_iota(jnp.int32, (clusters, firms), 0)
    member = jnp.where(cluster == ids_ref[...], 1.0, 0.0).astype(jnp.bfloat16)
    wide = fast(table, member, NN)
    wide_ref[...] = wide
    tall_ref[...] = wide.T


def first_kernel(start_ref, factor_ref, res_ref, out_ref, start_split):
    step = pl.program_id(0)
    copies, factors, width = out_ref.shape
    rows = res_ref.shape[0]
    firms = rows * STEPS

    @pl.when(step == 0)
    def _():
        start = start_ref[...]
        high = start.astype(jnp.bfloat16).astype(jnp.float32)
        both = jnp.concatenate([high, start - high], axis=0).astype(jnp.bfloat16)
        start_split[...] = jnp.zeros_like(start_split)
        start_split[0 : 2 * factors, :] = both
        small = exact(start, factor_ref[...], NT)
        small = jnp.concatenate([small, jnp.zeros((factors, width - firms - factors), jnp.float32)], axis=1)
        out_ref[:, :, firms:] = jnp.broadcast_to(small[None], (copies, factors, width - firms))

    high, low = split(res_ref[...])
    part = fast(high, start_split[...], NT) + fast(low, start_split[...], NT)
    part = part.T
    part = part[0:factors] + part[factors : 2 * factors]
    out_ref[:, :, pl.ds(pl.multiple_of(step * rows, rows), rows)] = jnp.broadcast_to(part[None], (copies, factors, rows))


def days_from(raw_t, signs_ref, loadings_ref, left_ref, small_ref):
    factors = loadings_ref.shape[0]
    n = raw_t.shape[0]
    high, low = split(signs_ref[...] * raw_t)
    left_ref[0:n] = high
    left_ref[n:] = low
    small_ref[...] = exact(raw_t, loadings_ref[...], NT)
    return compact(exact(raw_t, raw_t, NT), factors)


def days_tile(step, factor_ref, res_ref, left_ref, small_ref, send_ref, keep_ref):
    n = small_ref.shape[0]
    rows = send_ref.shape[1] - factor_ref.shape[0]
    high, low = split(res_ref[...])
    both = fast(left_ref[...], high, NN)
    tile = both[0:n] + both[n:] + fast(left_ref[0:n], low, NN) + exact(small_ref[...], factor_ref[...], NN)
    tile = tile.T
    tile = tile.reshape(tile.shape[0] // rows, rows, n)
    half = STEPS // 2
    at = pl.ds(lax.rem(step, half) * tile.shape[0], tile.shape[0])

    @pl.when(step < half)
    def _():
        send_ref[at, 0:rows, :] = tile

    @pl.when(step >= half)
    def _():
        keep_ref[at, 0:rows, :] = tile


def put_gram(gram, send_ref, keep_ref):
    copies, rows, n = send_ref.shape
    wide = jnp.broadcast_to(gram[None], (copies, gram.shape[0], n))
    send_ref[:, rows - gram.shape[0] :, :] = wide
    keep_ref[:, rows - gram.shape[0] :, :] = wide


def days_first_kernel(core_ref, got_ref, signs_ref, loadings_ref, factor_ref, res_ref, send_ref, keep_ref, left_ref, small_ref):
    step = pl.program_id(0)

    @pl.when(step == 0)
    def _():
        factors, firms = loadings_ref.shape
        n = signs_ref.shape[0]
        got = got_ref[...].sum(axis=0)
        by_residuals, mixed = got[:, 0:firms], got[:, firms : firms + factors]
        by_factors = jnp.zeros((factors, firms), jnp.float32)
        for m in range(factors):
            by_factors = by_factors + mixed[:, m : m + 1] * loadings_ref[m : m + 1, :]
        copies = n // factors
        raw_t = signs_ref[...] * jnp.concatenate([by_residuals] * copies, axis=0)
        raw_t = raw_t + jnp.concatenate([by_factors] * copies, axis=0)
        put_gram(days_from(raw_t, signs_ref, loadings_ref, left_ref, small_ref), send_ref, keep_ref)

    days_tile(step, factor_ref, res_ref, left_ref, small_ref, send_ref, keep_ref)


def days_later_kernel(core_ref, got_ref, gram_ref, signs_ref, loadings_ref, factor_ref, res_ref, send_ref, keep_ref, raw_ref, left_ref, small_ref):
    step = pl.program_id(0)

    @pl.when(step == 0)
    def _():
        raw = exact(got_ref[...], inverse_blocks(gram_ref[...], loadings_ref.shape[0]), NT)
        raw_ref[...] = raw
        put_gram(days_from(raw.T, signs_ref, loadings_ref, left_ref, small_ref), send_ref, keep_ref)

    days_tile(step, factor_ref, res_ref, left_ref, small_ref, send_ref, keep_ref)


def firms_kernel(core_ref, mine_ref, other_ref, gram_ref, signs_ref, loadings_ref, factor_ref, res_ref, out_ref, raw_ref, right_ref, add_ref):
    step = pl.program_id(0)
    factors = loadings_ref.shape[0]
    half, n = mine_ref.shape
    rows = res_ref.shape[0]

    @pl.when(step == 0)
    def _():
        inverse = inverse_blocks(gram_ref[...], factors)
        core = core_ref[0]
        raw_ref[pl.ds(pl.multiple_of(core * half, half), half), :] = exact(mine_ref[...], inverse, NT)
        raw_ref[pl.ds(pl.multiple_of((1 - core) * half, half), half), :] = exact(other_ref[...], inverse, NT)
        raw = raw_ref[...]
        high, low = split(raw)
        right_ref[:, 0:n] = high
        right_ref[:, n:] = low
        gram = compact(exact(raw, raw, TN), factors)
        copies, total = out_ref.shape[0], out_ref.shape[1]
        out_ref[:, total - factors :, :] = jnp.broadcast_to(gram[None], (copies, factors, n))
        add_ref[...] = exact(loadings_ref[...], exact(factor_ref[...], raw, NN), TN)

    high, low = split(res_ref[...])
    both = fast(high, right_ref[...], NN)
    part = both[:, 0:n] + both[:, n:] + fast(low, right_ref[:, 0:n], NN)
    at = pl.ds(pl.multiple_of(step * rows, rows), rows)
    part = signs_ref[at, :] * part + add_ref[at, :]
    block = out_ref.shape[1] - factors
    part = part.reshape(rows // block, block, n)
    out_ref[pl.ds(step * (rows // block), rows // block), 0:block, :] = part


def last_kernel(core_ref, mine_ref, other_ref, gram_ref, raw_ref, out_ref, inverse_ref):
    factors = gram_ref.shape[0]
    half, n = mine_ref.shape
    inverse = inverse_blocks(gram_ref[...], factors)
    inverse_ref[...] = inverse
    core = core_ref[0]
    raw_ref[pl.ds(pl.multiple_of(core * half, half), half), :] = exact(mine_ref[...], inverse, NT)
    raw_ref[pl.ds(pl.multiple_of((1 - core) * half, half), half), :] = exact(other_ref[...], inverse, NT)
    raw = raw_ref[...]
    out_ref[...] = jnp.broadcast_to(compact(exact(raw, raw, TN), factors)[None], out_ref.shape)


def loadings_kernel(raw_ref, inverse_ref, out_ref, *, scale):
    out_ref[...] = scale * exact(raw_ref[...], inverse_ref[...], NT)


def factors_kernel(got_ref, raw_ref, out_ref, *, scale):
    gram = got_ref[...].sum(axis=0)
    out_ref[...] = scale * exact(raw_ref[...], inverse_blocks(gram, gram.shape[0]), NT)


def shape(*dims):
    return jax.ShapeDtypeStruct(dims, jnp.float32)


def whole(*dims):
    return pl.BlockSpec(dims, lambda *_: (0,) * len(dims))


def on_device(residuals, loadings, factor_path, start_guess, cluster_ids, sign_bits, *, chips, total_firms, total_days, day_ranks):
    firms, days = residuals.shape
    factors = start_guess.shape[1]
    clusters, reps = sign_bits.shape
    n = reps * factors
    half = days // 2
    chunk = half // chips
    block = firms // day_ranks
    loadings_t, factor_t, start_t = loadings.T, factor_path.T, start_guess.T
    core = lax.axis_index("core").astype(jnp.int32).reshape(1)

    signs_t, signs = pl.pallas_call(
        functools.partial(signs_kernel, factors=factors),
        out_shape=(shape(n, firms), shape(firms, n)),
        compiler_params=PARAMS,
        name="signs",
    )(cluster_ids.reshape(1, firms), sign_bits.T)

    first = pl.pallas_call(
        first_kernel,
        grid=(STEPS,),
        in_specs=[whole(factors, days), whole(factors, days), pl.BlockSpec((firms // STEPS, days), lambda t: (t, 0))],
        out_specs=whole(day_ranks, factors, firms + n),
        out_shape=shape(day_ranks, factors, firms + n),
        scratch_shapes=[pltpu.VMEM((n, days), jnp.bfloat16)],
        compiler_params=PARAMS,
        name="first",
    )(start_t, factor_t, residuals)
    first = lax.all_to_all(first, ("x_hi", "y"), 0, 0, tiled=True)

    tiles = STEPS // 2

    def tile_of(t, core_ref):
        side = jnp.where(t < tiles, 1 - core_ref[0], core_ref[0])
        return side * tiles + lax.rem(t, tiles)

    day_specs = [
        pl.BlockSpec((factors, days // STEPS), lambda t, c: (0, tile_of(t, c))),
        pl.BlockSpec((firms, days // STEPS), lambda t, c: (0, tile_of(t, c))),
    ]
    day_scratch = [pltpu.VMEM((2 * n, firms), jnp.bfloat16), pltpu.VMEM((n, factors), jnp.float32)]
    parts = (chips, chunk + factors, n)

    def sum_firms(send, keep):
        pair = keep + lax.ppermute(send, "core", [(0, 1), (1, 0)])
        got = lax.all_to_all(pair, ("x_lo", "z"), 0, 0, tiled=True).sum(axis=0)
        mine = jnp.broadcast_to(got[None, 0:chunk], (chips, chunk, n))
        mine = lax.all_to_all(mine, ("x_lo", "z"), 0, 0, tiled=True).reshape(half, n)
        return mine, lax.ppermute(mine, "core", [(0, 1), (1, 0)]), got[chunk:]

    send, keep = pl.pallas_call(
        days_first_kernel,
        grid_spec=pltpu.PrefetchScalarGridSpec(
            num_scalar_prefetch=1,
            grid=(STEPS,),
            in_specs=[whole(day_ranks, factors, firms + n), whole(n, firms), whole(factors, firms), *day_specs],
            out_specs=[whole(*parts), whole(*parts)],
            scratch_shapes=day_scratch,
        ),
        out_shape=(shape(*parts), shape(*parts)),
        compiler_params=PARAMS,
        name="days_first",
    )(core, first, signs_t, loadings_t, factor_t, residuals)
    mine, other, gram = sum_firms(send, keep)

    by_day = pl.pallas_call(
        firms_kernel,
        grid_spec=pltpu.PrefetchScalarGridSpec(
            num_scalar_prefetch=1,
            grid=(STEPS,),
            in_specs=[
                whole(half, n),
                whole(half, n),
                whole(factors, n),
                whole(firms, n),
                whole(factors, firms),
                whole(factors, days),
                pl.BlockSpec((firms // STEPS, days), lambda t, c: (t, 0)),
            ],
            out_specs=whole(day_ranks, block + factors, n),
            scratch_shapes=[
                pltpu.VMEM((days, n), jnp.float32),
                pltpu.VMEM((days, 2 * n), jnp.bfloat16),
                pltpu.VMEM((firms, n), jnp.float32),
            ],
        ),
        out_shape=shape(day_ranks, block + factors, n),
        compiler_params=PARAMS,
        name="firms",
    )(core, mine, other, gram, signs, loadings_t, factor_t, residuals)
    got = lax.all_to_all(by_day, ("x_hi", "y"), 0, 0, tiled=True).sum(axis=0)
    gram = got[block:]
    wide = jnp.broadcast_to(got[None, 0:block], (day_ranks, block, n))
    wide = lax.all_to_all(wide, ("x_hi", "y"), 0, 0, tiled=True).reshape(firms, n)

    send, keep, raw_loads = pl.pallas_call(
        days_later_kernel,
        grid_spec=pltpu.PrefetchScalarGridSpec(
            num_scalar_prefetch=1,
            grid=(STEPS,),
            in_specs=[whole(firms, n), whole(factors, n), whole(n, firms), whole(factors, firms), *day_specs],
            out_specs=[whole(*parts), whole(*parts), whole(firms, n)],
            scratch_shapes=day_scratch,
        ),
        out_shape=(shape(*parts), shape(*parts), shape(firms, n)),
        compiler_params=PARAMS,
        name="days_later",
    )(core, wide, gram, signs_t, loadings_t, factor_t, residuals)
    mine, other, gram = sum_firms(send, keep)

    raw_factors, last, inverse = pl.pallas_call(
        last_kernel,
        in_specs=[pl.BlockSpec(memory_space=pltpu.SMEM)] + [pl.BlockSpec(memory_space=pltpu.VMEM)] * 3,
        out_shape=(shape(days, n), shape(day_ranks, factors, n), shape(n, n)),
        compiler_params=PARAMS,
        name="last",
    )(core, mine, other, gram)
    last = lax.all_to_all(last, ("x_hi", "y"), 0, 0, tiled=True)
    boot_loadings = pl.pallas_call(
        functools.partial(loadings_kernel, scale=math.sqrt(total_firms)),
        out_shape=shape(firms, n),
        compiler_params=PARAMS,
        name="boot_loadings",
    )(raw_loads, inverse)
    boot_factors = pl.pallas_call(
        functools.partial(factors_kernel, scale=math.sqrt(total_days)),
        out_shape=shape(days, n),
        compiler_params=PARAMS,
        name="boot_factors",
    )(last, raw_factors)
    return boot_loadings, boot_factors


def solution(mesh):
    firm_ranks, day_ranks = mesh.shape["firm"], mesh.shape["day"]
    axes = ("x_lo", "z", "core", "x_hi", "y")
    fine = Mesh(mesh.devices.reshape(2, firm_ranks // 4, 2, 2, day_ranks // 2), axes)
    firm, day = ("x_lo", "z", "core"), ("x_hi", "y")

    def run(residuals, *rest):
        total_firms, total_days = residuals.shape
        body = functools.partial(
            on_device, chips=firm_ranks // 2, total_firms=total_firms, total_days=total_days, day_ranks=day_ranks
        )
        return jax.shard_map(
            body,
            mesh=fine,
            in_specs=(P(firm, day), P(firm, None), P(day, None), P(day, None), P(firm), P()),
            out_specs=(P(firm, None), P(day, None)),
            check_vma=False,
        )(residuals, *rest)

    return run
```

time: 1080 us -> 195 us (0.18)
  waiting for transfers between devices: 615 us -> 27.4 us
  blocking collectives: 282 us -> 95.2 us
  other arithmetic: 87.7 us -> 0.27 us
  matrix products: 70.2 us -> 0 us
  Pallas kernels: 0 us -> 40.9 us
  starting transfers between devices: 0.34 us -> 27.5 us
  between operations: 14 us -> 0.77 us
    psum x4 -> x0, waiting for transfers between devices: 615 us -> none  [the longest x2 442 us: on_device(): lax.psum(product + jnp.dot(factor_path, jnp.dot(loadings.T, loads_now, pr...]
    psum x4 -> x0, blocking collectives: 282 us -> none  [the longest x2 212 us: on_device(): normalize_gram_sum = lax.psum(gram_of(raw_loads), 'firm')]
    all_to_all x0 -> x5, blocking collectives: none -> 95.2 us  [the longest x2 46.5 us: sum_firms(): got = lax.all_to_all(pair, ('x_lo', 'z'), 0, 0, tiled=True).sum(axis=0)]
    another operation x22 -> x0, other arithmetic: 87.7 us -> none  [the longest x13 47.3 us: inverse_factor(): lower = jnp.linalg.cholesky(gram_sum)]
    dot_general x21 -> x0, matrix products: 68.7 us -> none  [the longest x2 22.6 us: on_device(): jnp.dot(residuals, current, precision=highest)]
    pallas_call x0 -> x8, Pallas kernels: none -> 40.9 us  [the longest x1 10.1 us: on_device(): pl.pallas_call(firms_kernel, grid_spec=pltpu.PrefetchScalarGridSpec(num_s...]
    all_to_all x0 -> x3, waiting for transfers between devices: none -> 21.1 us  [the longest x1 8.66 us: on_device(): lax.all_to_all(wide, ('x_hi', 'y'), 0, 0, tiled=True).reshape(firms, n)]
    all_to_all x0 -> x3, starting transfers between devices: none -> 14.3 us  [the longest x1 7.48 us: on_device(): first = lax.all_to_all(first, ('x_hi', 'y'), 0, 0, tiled=True)]
  transfers between devices with their start and end apart: 4 -> 7, of which waited for: 4 -> 7; matrix products, arithmetic and copies ran while one was open for 0% -> 0% of each run, Pallas kernels for 0% -> 1%
where the time goes in v1:
time: 195 us
  blocking collectives  95.2 us (49%)
  Pallas kernels  40.9 us (21%)
  starting transfers between devices  27.5 us (14%)
  waiting for transfers between devices  27.4 us (14%)
  local copies, waits for them, and re-layouts  2.62 us (1%)
    all_to_all x2, blocking collectives, sum_firms(): got = lax.all_to_all(pair, ('x_lo', 'z'), 0, 0, tiled=True).sum(axis=0)  46.5 us
    all_to_all x2, blocking collectives, sum_firms(): lax.all_to_all(mine, ('x_lo', 'z'), 0, 0, tiled=True).reshape(half, n)  34.2 us
    all_to_all x1, blocking collectives, on_device(): got = lax.all_to_all(by_day, ('x_hi', 'y'), 0, 0, tiled=True).sum(axis=0)  14.5 us
    pallas_call x1, Pallas kernels, on_device(): pl.pallas_call(firms_kernel, grid_spec=pltpu.PrefetchScalarGridSpec(num_s...  10.1 us
    pallas_call x1, Pallas kernels, on_device(): pl.pallas_call(days_later_kernel, grid_spec=pltpu.PrefetchScalarGridSpec(...  9.13 us
    all_to_all x1, waiting for transfers between devices, on_device(): lax.all_to_all(wide, ('x_hi', 'y'), 0, 0, tiled=True).reshape(firms, n)  8.66 us
    all_to_all x1, starting transfers between devices, on_device(): first = lax.all_to_all(first, ('x_hi', 'y'), 0, 0, tiled=True)  7.48 us
    all_to_all x1, waiting for transfers between devices, on_device(): first = lax.all_to_all(first, ('x_hi', 'y'), 0, 0, tiled=True)  7.26 us
  transfers between devices with their start and end apart: 7, of which 7 were waited for; matrix products, arithmetic and copies ran while one was open for 0% of the time, Pallas kernels for 1%

profile of v1, /device:TPU:1, one launch (start us, length us, event | category | flops | bytes accessed | tf_op | source)
XLA Modules:
  0.0 194.7 jit_solution(8402463037256304080)
XLA Ops:
  2.3 6.6 %first.1 = f32[8,8,1152]{2,1,0:T(8,128)} custom-call(f32[8,2048]{1,0:T(8,128)S(1)} %bitcast.21, f32[8,2048]{1,0:T(8,128)S(1)} %bitcast.14, f32[1024,2048]{1,0:T(8,128)} %res_ref.7), custom_call_target="tpu_custom_call" | custom-call | tf_op jit(solution)/shard_map/first/pallas_call | solution.py:245
  9.0 7.5 %all-to-all-start = ((f32[8,8,1152]{2,1,0:T(8,128)}), f32[8,8,1152]{2,1,0:T(8,128)S(1)}, u32[]{:S(2)}, u32[]{:S(2)}) async-start(f32[8,8,1152]{2,1,0:T(8,128)} %first.1), calls=%async_computation | async-start | bytes 589824 | tf_op jit(solution)/shard_map/all_to_all | solution.py:255
  16.9 7.3 %all-to-all-done.got_ref = f32[8,8,1152]{2,1,0:T(8,128)S(1)} async-done(((f32[8,8,1152]{2,1,0:T(8,128)}), f32[8,8,1152]{2,1,0:T(8,128)S(1)}, u32[]{:S(2)}, u32[]{:S(2)}) %all-to-all-start) | async-done | bytes 294944 | tf_op jit(solution)/shard_map/all_to_all | solution.py:255
  24.2 7.2 %days_first.1 = (f32[16,72,128]{2,1,0:T(8,128)S(1)}, f32[16,72,128]{2,1,0:T(8,128)S(1)}) custom-call(s32[1]{0:T(128)} %bitcast.core_ref, f32[8,8,1152]{2,1,0:T(8,128)S(1)} %all-to-all-done.got_ref, f32[128,1024]{1,0:T(8,128)S(1)} %get-tuple-element.12.signs_ref, f32[8,1024]{1,0:T(8,128)S(1)} %bitcast.18, f32[8,2048]{1,0:T(8,128)S(1)} %bitcast.15, ...), custom_call_target="tpu_custom_call" | custom-call | tf_op jit(solution)/shard_map/days_first/pallas_call | solution.py:277
  31.4 2.4 %collective-permute-start = (f32[16,72,128]{2,1,0:T(8,128)S(1)}, f32[16,72,128]{2,1,0:T(8,128)S(1)}, u32[]{:S(2)}, u32[]{:S(2)}) collective-permute-start(f32[16,72,128]{2,1,0:T(8,128)S(1)} %get-tuple-element.14), channel_id=1, source_target_pairs={{0,8},{8,0},{1,9},{9,1},{2,10},{10,2},{3,11},{11,3},{4,12},{12,4},... | collective-permute-start | bytes 1769480 | tf_op jit(solution)/shard_map/ppermute | solution.py:271
  33.8 1.6 collective-permute-done
  35.5 25.4 %all_to_all.40 = f32[16,72,128]{2,1,0:T(8,128)S(1)} all-to-all(f32[16,72,128]{2,1,0:T(8,128)S(1)} %add.6), channel_id=1, replica_groups=mesh['x_lo'=2,'z'=8,'core'=2,'x_hi'=2,'y'=4] {'x_lo','z'}, dimensions={0} | all-to-all | bytes 1179648 | tf_op jit(solution)/shard_map/all_to_all | solution.py:272
  61.0 17.1 %all_to_all.41 = f32[16,64,128]{2,1,0:T(8,128)S(1)} all-to-all(f32[16,64,128]{2,1,0:T(8,128)S(1)} %broadcast_in_dim.6), channel_id=1, replica_groups=mesh['x_lo'=2,'z'=8,'core'=2,'x_hi'=2,'y'=4] {'x_lo','z'}, dimensions={0} | all-to-all | bytes 1048576 | tf_op jit(solution)/shard_map/all_to_all | solution.py:274
  78.1 3.6 %collective-permute-start.1 = (f32[1024,128]{1,0:T(8,128)S(1)}, f32[1024,128]{1,0:T(8,128)S(1)}, u32[]{:S(2)}, u32[]{:S(2)}) collective-permute-start(f32[1024,128]{1,0:T(8,128)S(1)} %bitcast.10), channel_id=1, source_target_pairs={{0,8},{8,0},{1,9},{9,1},{2,10},{10,2},{3,11},{11,3},{4,12},{12,4},... | collective-permute-start | bytes 1572872 | tf_op jit(solution)/shard_map/ppermute | solution.py:275
  83.2 10.1 %firms.1 = f32[8,136,128]{2,1,0:T(8,128)S(1)} custom-call(s32[1]{0:T(128)} %bitcast.core_ref, f32[1024,128]{1,0:T(8,128)S(1)} %bitcast.11, f32[1024,128]{1,0:T(8,128)S(1)} %collective-permute-done.1.other_ref, f32[8,128]{1,0:T(8,128)S(1)} %slice.25.gram_ref, f32[1024,128]{1,0:T(8,128)S(1)} %get-tuple-element.15.signs_ref, f32[8,1024]{1,0:T(8,128)S(1)} %bitcast.19, ...), custom_call_target="tpu_custom_call" | custom-call | tf_op jit(solution)/shard_map/firms/pallas_call | solution.py:292
  93.3 14.5 %all_to_all.42 = f32[8,136,128]{2,1,0:T(8,128)S(1)} all-to-all(f32[8,136,128]{2,1,0:T(8,128)S(1)} %firms.1), channel_id=1, replica_groups=mesh['x_lo'=2,'z'=8,'core'=2,'x_hi'=2,'y'=4] {'x_hi','y'}, dimensions={0} | all-to-all | bytes 1114112 | tf_op jit(solution)/shard_map/all_to_all | solution.py:317
  108.6 3.5 %all-to-all-start.4 = ((f32[8,128,128]{2,1,0:T(8,128)}), f32[8,128,128]{2,1,0:T(8,128)S(1)}, u32[]{:S(2)}, u32[]{:S(2)}) async-start(f32[8,128,128]{2,1,0:T(8,128)} %broadcast_in_dim.7), calls=%async_computation.4 | async-start | bytes 1048576 | tf_op jit(solution)/shard_map/all_to_all | solution.py:320
  112.2 8.7 %all-to-all-done.4 = f32[8,128,128]{2,1,0:T(8,128)S(1)} async-done(((f32[8,128,128]{2,1,0:T(8,128)}), f32[8,128,128]{2,1,0:T(8,128)S(1)}, u32[]{:S(2)}, u32[]{:S(2)}) %all-to-all-start.4) | async-done | bytes 524320 | tf_op jit(solution)/shard_map/all_to_all | solution.py:320
  120.8 9.1 %days_later.1 = (f32[16,72,128]{2,1,0:T(8,128)S(1)}, f32[16,72,128]{2,1,0:T(8,128)S(1)}, f32[1024,128]{1,0:T(8,128)S(1)}) custom-call(s32[1]{0:T(128)} %bitcast.core_ref, f32[1024,128]{1,0:T(8,128)S(1)} %bitcast.9, f32[8,128]{1,0:T(8,128)S(1)} %slice.27.gram_ref, f32[128,1024]{1,0:T(8,128)S(1)} %get-tuple-element.12.signs_ref, f32[8,1024]{1,0:T(8,128)S(1)} %bitcast.20, ...), custom_call_target="tpu_custom_call" | custom-call | tf_op jit(solution)/shard_map/days_later/pallas_call | solution.py:322
  130.0 3.7 %collective-permute-start.2 = (f32[16,72,128]{2,1,0:T(8,128)S(1)}, f32[16,72,128]{2,1,0:T(8,128)S(1)}, u32[]{:S(2)}, u32[]{:S(2)}) collective-permute-start(f32[16,72,128]{2,1,0:T(8,128)S(1)} %get-tuple-element.18), channel_id=1, source_target_pairs={{0,8},{8,0},{1,9},{9,1},{2,10},{10,2},{3,11},{11,3},{4,12},{12,4},... | collective-permute-start | bytes 1769480 | tf_op jit(solution)/shard_map/ppermute | solution.py:271
  133.6 1.6 collective-permute-done.2
  135.3 21.1 %all_to_all.43 = f32[16,72,128]{2,1,0:T(8,128)S(1)} all-to-all(f32[16,72,128]{2,1,0:T(8,128)S(1)} %add.7), channel_id=1, replica_groups=mesh['x_lo'=2,'z'=8,'core'=2,'x_hi'=2,'y'=4] {'x_lo','z'}, dimensions={0} | all-to-all | bytes 1179648 | tf_op jit(solution)/shard_map/all_to_all | solution.py:272
  156.6 17.1 %all_to_all.44 = f32[16,64,128]{2,1,0:T(8,128)S(1)} all-to-all(f32[16,64,128]{2,1,0:T(8,128)S(1)} %broadcast_in_dim.8), channel_id=1, replica_groups=mesh['x_lo'=2,'z'=8,'core'=2,'x_hi'=2,'y'=4] {'x_lo','z'}, dimensions={0} | all-to-all | bytes 1048576 | tf_op jit(solution)/shard_map/all_to_all | solution.py:274
  173.7 3.6 %collective-permute-start.3 = (f32[1024,128]{1,0:T(8,128)S(1)}, f32[1024,128]{1,0:T(8,128)S(1)}, u32[]{:S(2)}, u32[]{:S(2)}) collective-permute-start(f32[1024,128]{1,0:T(8,128)S(1)} %bitcast.12), channel_id=1, source_target_pairs={{0,8},{8,0},{1,9},{9,1},{2,10},{10,2},{3,11},{11,3},{4,12},{12,4},... | collective-permute-start | bytes 1572872 | tf_op jit(solution)/shard_map/ppermute | solution.py:275
  177.3 1.5 collective-permute-done.3.other_ref
  178.8 3.4 %last.1 = (f32[2048,128]{1,0:T(8,128)S(1)}, f32[8,8,128]{2,1,0:T(8,128)}, f32[128,128]{1,0:T(8,128)S(1)}) custom-call(s32[1]{0:T(128)} %bitcast.core_ref, f32[1024,128]{1,0:T(8,128)S(1)} %bitcast.13, f32[1024,128]{1,0:T(8,128)S(1)} %collective-permute-done.3.other_ref, f32[8,128]{1,0:T(8,128)S(1)} %slice.29.gram_ref), custom_call_target="tpu_custom_call" | custom-call | tf_op jit(solution)/shard_map/last/pallas_call | solution.py:337
  182.2 3.3 %all-to-all-start.7 = ((f32[8,8,128]{2,1,0:T(8,128)}), f32[8,8,128]{2,1,0:T(8,128)S(1)}, u32[]{:S(2)}, u32[]{:S(2)}) async-start(f32[8,8,128]{2,1,0:T(8,128)} %get-tuple-element.20), calls=%async_computation.7 | async-start | bytes 65536 | tf_op jit(solution)/shard_map/all_to_all | solution.py:344
  186.9 5.2 %all-to-all-done.7.got_ref = f32[8,8,128]{2,1,0:T(8,128)S(1)} async-done(((f32[8,8,128]{2,1,0:T(8,128)}), f32[8,8,128]{2,1,0:T(8,128)S(1)}, u32[]{:S(2)}, u32[]{:S(2)}) %all-to-all-start.7) | async-done | bytes 32800 | tf_op jit(solution)/shard_map/all_to_all | solution.py:344
  192.1 2.6 %boot_factors.1 = f32[2048,128]{1,0:T(8,128)} custom-call(f32[8,8,128]{2,1,0:T(8,128)S(1)} %all-to-all-done.7.got_ref, f32[2048,128]{1,0:T(8,128)S(1)} %get-tuple-element.21.raw_ref), custom_call_target="tpu_custom_call" | custom-call | tf_op jit(solution)/shard_map/boot_factors/pallas_call | solution.py:351
  (29 shorter events, 6.2 us)
Async XLA Ops:
  0.6 0.8 copy-start
  1.5 0.8 copy-start.3
  2.3 14.1 %copy-start.4 = (s32[512,16]{0,1:T(8,128)S(1)}, s32[512,16]{0,1:T(8,128)}, u32[]{:S(2)}) copy-start(s32[512,16]{0,1:T(8,128)} %param.11) | copy-start | bytes 98308
  2.3 14.1 %copy-start.5 = (s32[1024]{0:T(1024)S(1)}, s32[1024]{0:T(1024)}, u32[]{:S(2)}) copy-start(s32[1024]{0:T(1024)} %param.10) | copy-start | bytes 12292
  2.3 21.8 %copy-start.1 = (f32[2048,8]{0,1:T(8,128)S(1)}, f32[2048,8]{0,1:T(8,128)}, u32[]{:S(2)}) copy-start(f32[2048,8]{0,1:T(8,128)} %param.8) | copy-start | bytes 196612
  2.3 21.8 %copy-start.2 = (f32[1024,8]{0,1:T(8,128)S(1)}, f32[1024,8]{0,1:T(8,128)}, u32[]{:S(2)}) copy-start(f32[1024,8]{0,1:T(8,128)} %param.7) | copy-start | bytes 98308
  9.0 15.2 %all-to-all-start = ((f32[8,8,1152]{2,1,0:T(8,128)}), f32[8,8,1152]{2,1,0:T(8,128)S(1)}, u32[]{:S(2)}, u32[]{:S(2)}) async-start(f32[8,8,1152]{2,1,0:T(8,128)} %first.1), calls=%async_computation | async-start | bytes 589824 | tf_op jit(solution)/shard_map/all_to_all | solution.py:255
  31.4 4.0 %collective-permute-start = (f32[16,72,128]{2,1,0:T(8,128)S(1)}, f32[16,72,128]{2,1,0:T(8,128)S(1)}, u32[]{:S(2)}, u32[]{:S(2)}) collective-permute-start(f32[16,72,128]{2,1,0:T(8,128)S(1)} %get-tuple-element.14), channel_id=1, source_target_pairs={{0,8},{8,0},{1,9},{9,1},{2,10},{10,2},{3,11},{11,3},{4,12},{12,4},... | collective-permute-start | bytes 1769480 | tf_op jit(solution)/shard_map/ppermute | solution.py:271
  78.1 5.1 %collective-permute-start.1 = (f32[1024,128]{1,0:T(8,128)S(1)}, f32[1024,128]{1,0:T(8,128)S(1)}, u32[]{:S(2)}, u32[]{:S(2)}) collective-permute-start(f32[1024,128]{1,0:T(8,128)S(1)} %bitcast.10), channel_id=1, source_target_pairs={{0,8},{8,0},{1,9},{9,1},{2,10},{10,2},{3,11},{11,3},{4,12},{12,4},... | collective-permute-start | bytes 1572872 | tf_op jit(solution)/shard_map/ppermute | solution.py:275
  108.6 12.2 %all-to-all-start.4 = ((f32[8,128,128]{2,1,0:T(8,128)}), f32[8,128,128]{2,1,0:T(8,128)S(1)}, u32[]{:S(2)}, u32[]{:S(2)}) async-start(f32[8,128,128]{2,1,0:T(8,128)} %broadcast_in_dim.7), calls=%async_computation.4 | async-start | bytes 1048576 | tf_op jit(solution)/shard_map/all_to_all | solution.py:320
  130.0 5.3 %collective-permute-start.2 = (f32[16,72,128]{2,1,0:T(8,128)S(1)}, f32[16,72,128]{2,1,0:T(8,128)S(1)}, u32[]{:S(2)}, u32[]{:S(2)}) collective-permute-start(f32[16,72,128]{2,1,0:T(8,128)S(1)} %get-tuple-element.18), channel_id=1, source_target_pairs={{0,8},{8,0},{1,9},{9,1},{2,10},{10,2},{3,11},{11,3},{4,12},{12,4},... | collective-permute-start | bytes 1769480 | tf_op jit(solution)/shard_map/ppermute | solution.py:271
  173.7 5.1 %collective-permute-start.3 = (f32[1024,128]{1,0:T(8,128)S(1)}, f32[1024,128]{1,0:T(8,128)S(1)}, u32[]{:S(2)}, u32[]{:S(2)}) collective-permute-start(f32[1024,128]{1,0:T(8,128)S(1)} %bitcast.12), channel_id=1, source_target_pairs={{0,8},{8,0},{1,9},{9,1},{2,10},{10,2},{3,11},{11,3},{4,12},{12,4},... | collective-permute-start | bytes 1572872 | tf_op jit(solution)/shard_map/ppermute | solution.py:275
  182.2 9.9 %all-to-all-start.7 = ((f32[8,8,128]{2,1,0:T(8,128)}), f32[8,8,128]{2,1,0:T(8,128)S(1)}, u32[]{:S(2)}, u32[]{:S(2)}) async-start(f32[8,8,128]{2,1,0:T(8,128)} %get-tuple-element.20), calls=%async_computation.7 | async-start | bytes 65536 | tf_op jit(solution)/shard_map/all_to_all | solution.py:344

commit v2 on v1

v2 whole, which is shorter than its diff:
```python
import functools
import math

import jax
import jax.numpy as jnp
from jax import lax
from jax.experimental import pallas as pl
from jax.experimental.pallas import tpu as pltpu
from jax.sharding import Mesh
from jax.sharding import PartitionSpec as P

STEPS = 4
AHEAD = 4
HIGHEST = lax.Precision.HIGHEST
NN = (((1,), (0,)), ((), ()))
NT = (((1,), (1,)), ((), ()))
TN = (((0,), (0,)), ((), ()))
PARAMS = pltpu.CompilerParams(vmem_limit_bytes=32 * 1024 * 1024)


def exact(a, b, dims):
    return lax.dot_general(a, b, dims, precision=HIGHEST, preferred_element_type=jnp.float32)


def fast(a, b, dims):
    return lax.dot_general(a, b, dims, preferred_element_type=jnp.float32)


def split(x):
    high = x.astype(jnp.bfloat16)
    return high, (x - high.astype(jnp.float32)).astype(jnp.bfloat16)


def compact(full, factors):
    n = full.shape[0]
    row = lax.broadcasted_iota(jnp.int32, (n, n), 0) // factors
    lane = lax.broadcasted_iota(jnp.int32, (n, n), 1) // factors
    kept = jnp.where(row == lane, full, 0.0)
    return kept.reshape(n // factors, factors, n).sum(axis=0)


def inverse_blocks(gram, factors):
    n = gram.shape[1]
    row = lax.broadcasted_iota(jnp.int32, (factors, n), 0)
    lane = lax.broadcasted_iota(jnp.int32, (factors, n), 1)
    first = (lane // factors) * factors
    rest = gram
    inverse = jnp.where(row == lane - first, 1.0, 0.0)
    for j in range(factors):
        column = jnp.take_along_axis(rest, first + j, axis=1, mode="promise_in_bounds")
        pivot = column[j : j + 1]
        ratio = jnp.where(row > j, column / pivot, 0.0)
        rest = rest - ratio * rest[j : j + 1]
        inverse = inverse - ratio * inverse[j : j + 1]
        inverse = jnp.where(row == j, inverse / jnp.sqrt(pivot), inverse)
    wide = jnp.concatenate([inverse] * (n // factors), axis=0)
    row = lax.broadcasted_iota(jnp.int32, (n, n), 0) // factors
    lane = lax.broadcasted_iota(jnp.int32, (n, n), 1) // factors
    return jnp.where(row == lane, wide, 0.0)


def put_signs(ids_ref, bits_ref, wide_ref, tall_ref):
    reps, clusters = bits_ref.shape
    n, firms = wide_ref.shape
    table = 2.0 * bits_ref[...].astype(jnp.float32) - 1.0
    table = jnp.broadcast_to(table[:, None, :], (reps, n // reps, clusters))
    table = table.reshape(n, clusters).astype(jnp.bfloat16)
    cluster = lax.broadcasted_iota(jnp.int32, (clusters, firms), 0)
    member = jnp.where(cluster == ids_ref[...], 1.0, 0.0).astype(jnp.bfloat16)
    wide = fast(table, member, NN)
    wide_ref[...] = wide
    tall_ref[...] = wide.T


def columns(t, width):
    return (slice(None), slice(t * width, (t + 1) * width))


def rows_of(t, rows):
    return (slice(t * rows, (t + 1) * rows), slice(None))


def bring(res_any, res_ref, sems, tiles):
    copies = [pltpu.make_async_copy(res_any.at[tile], res_ref.at[tile], sems.at[t]) for t, tile in enumerate(tiles)]
    for copy in copies[:AHEAD]:
        copy.start()
    return copies


def arrive(copies, t):
    copies[t].wait()
    if t + AHEAD < len(copies):
        copies[t + AHEAD].start()


def first_kernel(
    start_any, factor_any, ids_any, bits_any, res_any,
    out_ref, wide_ref, tall_ref,
    start_ref, factor_ref, ids_ref, bits_ref, res_ref, total_ref, sems,
):
    copies, factors, width = out_ref.shape
    firms, days = res_ref.shape
    n = total_ref.shape[1]
    pairs = [(start_any, start_ref), (factor_any, factor_ref), (ids_any, ids_ref), (bits_any, bits_ref)]
    small = [pltpu.make_async_copy(a, b, sems.at[STEPS + i]) for i, (a, b) in enumerate(pairs)]
    for copy in small:
        copy.start()
    tiles = [columns(t, days // STEPS) for t in range(STEPS)]
    large = bring(res_any, res_ref, sems, tiles)
    for copy in small:
        copy.wait()
    start = start_ref[...]
    high = start.astype(jnp.bfloat16).astype(jnp.float32)
    both = jnp.concatenate([high, start - high, jnp.zeros((n - 2 * factors, days), jnp.float32)], axis=0)
    both = both.T.astype(jnp.bfloat16)
    mixed = exact(start, factor_ref[...], NT)
    mixed = jnp.concatenate([mixed, jnp.zeros((factors, width - firms - factors), jnp.float32)], axis=1)
    out_ref[:, :, firms:] = jnp.broadcast_to(mixed[None], (copies, factors, width - firms))
    put_signs(ids_ref, bits_ref, wide_ref, tall_ref)
    for t in range(STEPS):
        arrive(large, t)
        high, low = split(res_ref[tiles[t]])
        right = both[t * (days // STEPS) : (t + 1) * (days // STEPS)]
        part = fast(high, right, NN) + fast(low, right, NN)
        total_ref[...] = part if t == 0 else total_ref[...] + part
    total = total_ref[...].T
    total = total[0:factors] + total[factors : 2 * factors]
    out_ref[:, :, 0:firms] = jnp.broadcast_to(total[None], (copies, factors, firms))


def days_from(raw_t, signs_ref, loadings_ref, left_ref, small_ref):
    factors = loadings_ref.shape[0]
    n = raw_t.shape[0]
    high, low = split(signs_ref[...] * raw_t)
    left_ref[0:n] = high
    left_ref[n:] = low
    small_ref[...] = exact(raw_t, loadings_ref[...], NT)
    return compact(exact(raw_t, raw_t, NT), factors)


def days_tiles(core, copies, tiles, factor_ref, res_ref, left_ref, small_ref, send_ref, keep_ref):
    n = small_ref.shape[0]
    rows = send_ref.shape[1] - factor_ref.shape[0]
    width = res_ref.shape[1] // STEPS
    half = STEPS // 2
    for t in range(STEPS):
        arrive(copies, t)
        high, low = split(res_ref[tiles[t]])
        both = fast(left_ref[...], high, NN)
        tile = both[0:n] + both[n:] + fast(left_ref[0:n], low, NN) + exact(small_ref[...], factor_ref[tiles[t]], NN)
        tile = tile.T.reshape(width // rows, rows, n)
        at = slice(t % half * (width // rows), (t % half + 1) * (width // rows))

        @pl.when(core != t // half)
        def _():
            send_ref[at, 0:rows, :] = tile

        @pl.when(core == t // half)
        def _():
            keep_ref[at, 0:rows, :] = tile


def put_gram(gram, send_ref, keep_ref):
    copies, rows, n = send_ref.shape
    wide = jnp.broadcast_to(gram[None], (copies, gram.shape[0], n))
    send_ref[:, rows - gram.shape[0] :, :] = wide
    keep_ref[:, rows - gram.shape[0] :, :] = wide


def days_first_kernel(core_ref, got_ref, signs_ref, loadings_ref, factor_ref, res_any, send_ref, keep_ref, left_ref, small_ref, res_ref, sems):
    tiles = [columns(t, res_ref.shape[1] // STEPS) for t in range(STEPS)]
    copies = bring(res_any, res_ref, sems, tiles)
    factors, firms = loadings_ref.shape
    n = signs_ref.shape[0]
    got = got_ref[...].sum(axis=0)
    by_residuals, mixed = got[:, 0:firms], got[:, firms : firms + factors]
    by_factors = jnp.zeros((factors, firms), jnp.float32)
    for m in range(factors):
        by_factors = by_factors + mixed[:, m : m + 1] * loadings_ref[m : m + 1, :]
    reps = n // factors
    raw_t = signs_ref[...] * jnp.concatenate([by_residuals] * reps, axis=0)
    raw_t = raw_t + jnp.concatenate([by_factors] * reps, axis=0)
    put_gram(days_from(raw_t, signs_ref, loadings_ref, left_ref, small_ref), send_ref, keep_ref)
    days_tiles(core_ref[0], copies, tiles, factor_ref, res_ref, left_ref, small_ref, send_ref, keep_ref)


def days_later_kernel(core_ref, got_ref, signs_ref, loadings_ref, factor_ref, res_any, send_ref, keep_ref, left_ref, small_ref, res_ref, sems):
    tiles = [columns(t, res_ref.shape[1] // STEPS) for t in range(STEPS)]
    copies = bring(res_any, res_ref, sems, tiles)
    put_gram(days_from(got_ref[...].T, signs_ref, loadings_ref, left_ref, small_ref), send_ref, keep_ref)
    days_tiles(core_ref[0], copies, tiles, factor_ref, res_ref, left_ref, small_ref, send_ref, keep_ref)


def firms_kernel(core_ref, mine_ref, other_ref, signs_ref, loadings_ref, factor_ref, res_any, out_ref, raw_ref, right_ref, add_ref, res_ref, sems):
    factors = loadings_ref.shape[0]
    half, n = mine_ref.shape
    rows = res_ref.shape[0] // STEPS
    tiles = [rows_of(t, rows) for t in range(STEPS)]
    large = bring(res_any, res_ref, sems, tiles)
    core = core_ref[0]
    raw_ref[pl.ds(pl.multiple_of(core * half, half), half), :] = mine_ref[...]
    raw_ref[pl.ds(pl.multiple_of((1 - core) * half, half), half), :] = other_ref[...]
    raw = raw_ref[...]
    high, low = split(raw)
    right_ref[:, 0:n] = high
    right_ref[:, n:] = low
    gram = compact(exact(raw, raw, TN), factors)
    copies, total = out_ref.shape[0], out_ref.shape[1]
    out_ref[:, total - factors :, :] = jnp.broadcast_to(gram[None], (copies, factors, n))
    add_ref[...] = exact(loadings_ref[...], exact(factor_ref[...], raw, NN), TN)
    block = total - factors
    for t in range(STEPS):
        arrive(large, t)
        at = slice(t * rows, (t + 1) * rows)
        high, low = split(res_ref[at, :])
        both = fast(high, right_ref[...], NN)
        part = both[:, 0:n] + both[:, n:] + fast(low, right_ref[:, 0:n], NN)
        part = signs_ref[at, :] * part + add_ref[at, :]
        out_ref[t * rows // block : (t + 1) * rows // block, 0:block, :] = part.reshape(rows // block, block, n)


def turn_kernel(got_ref, out_ref, inverse_ref):
    copies, rows, _ = out_ref.shape
    total = got_ref[...].sum(axis=0)
    inverse = inverse_blocks(total[rows:], total.shape[0] - rows)
    inverse_ref[...] = inverse
    chunk = exact(total[0:rows], inverse, NT)
    out_ref[...] = jnp.broadcast_to(chunk[None], out_ref.shape)


def last_kernel(core_ref, mine_ref, other_ref, raw_ref, out_ref):
    half = mine_ref.shape[0]
    mine, other = mine_ref[...], other_ref[...]
    core = core_ref[0]
    raw_ref[pl.ds(pl.multiple_of(core * half, half), half), :] = mine
    raw_ref[pl.ds(pl.multiple_of((1 - core) * half, half), half), :] = other
    gram = compact(exact(mine, mine, TN) + exact(other, other, TN), out_ref.shape[1])
    out_ref[...] = jnp.broadcast_to(gram[None], out_ref.shape)


def loadings_kernel(raw_ref, inverse_ref, out_ref, *, scale):
    out_ref[...] = scale * exact(raw_ref[...], inverse_ref[...], NT)


def factors_kernel(got_ref, raw_ref, out_ref, *, scale):
    gram = got_ref[...].sum(axis=0)
    out_ref[...] = scale * exact(raw_ref[...], inverse_blocks(gram, gram.shape[0]), NT)


def shape(*dims):
    return jax.ShapeDtypeStruct(dims, jnp.float32)


def inputs(count):
    small = [pl.BlockSpec(memory_space=pltpu.VMEM)] * count
    return [pl.BlockSpec(memory_space=pltpu.SMEM), *small]


def in_hbm(x):
    return pltpu.with_memory_space_constraint(x, pltpu.HBM)


def on_device(residuals, loadings, factor_path, start_guess, cluster_ids, sign_bits, *, chips, total_firms, total_days, day_ranks):
    firms, days = residuals.shape
    factors = start_guess.shape[1]
    clusters, reps = sign_bits.shape
    n = reps * factors
    half = days // 2
    chunk = half // chips
    block = firms // day_ranks
    loadings_t, factor_t, start_t = loadings.T, factor_path.T, start_guess.T
    core = lax.axis_index("core").astype(jnp.int32).reshape(1)

    residuals = in_hbm(residuals)
    block_scratch = [pltpu.VMEM((firms, days), jnp.float32), pltpu.SemaphoreType.DMA((STEPS,))]
    first, signs_t, signs = pl.pallas_call(
        first_kernel,
        in_specs=[pl.BlockSpec(memory_space=pl.ANY)] * 5,
        out_shape=(
            shape(day_ranks, factors, firms + n),
            shape(n, firms),
            shape(firms, n),
        ),
        scratch_shapes=[
            pltpu.VMEM((factors, days), jnp.float32),
            pltpu.VMEM((factors, days), jnp.float32),
            pltpu.VMEM((1, firms), jnp.int32),
            pltpu.VMEM((reps, clusters), jnp.int32),
            pltpu.VMEM((firms, days), jnp.float32),
            pltpu.VMEM((firms, n), jnp.float32),
            pltpu.SemaphoreType.DMA((STEPS + 4,)),
        ],
        compiler_params=PARAMS,
        name="first",
    )(in_hbm(start_t), in_hbm(factor_t), in_hbm(cluster_ids.reshape(1, firms)), in_hbm(sign_bits.T), residuals)
    first = lax.all_to_all(first, ("x_hi", "y"), 0, 0, tiled=True)

    day_scratch = [pltpu.VMEM((2 * n, firms), jnp.bfloat16), pltpu.VMEM((n, factors), jnp.float32), *block_scratch]
    parts = (chips, chunk + factors, n)

    def turn(got, rows):
        return pl.pallas_call(
            turn_kernel,
            out_shape=(shape(got.shape[0], rows, n), shape(n, n)),
            compiler_params=PARAMS,
            name="turn",
        )(got)

    def sum_firms(send, keep):
        pair = keep + lax.ppermute(send, "core", [(0, 1), (1, 0)])
        mine, inverse = turn(lax.all_to_all(pair, ("x_lo", "z"), 0, 0, tiled=True), chunk)
        mine = lax.all_to_all(mine, ("x_lo", "z"), 0, 0, tiled=True).reshape(half, n)
        return mine, lax.ppermute(mine, "core", [(0, 1), (1, 0)]), inverse

    send, keep = pl.pallas_call(
        days_first_kernel,
        in_specs=inputs(4) + [pl.BlockSpec(memory_space=pl.ANY)],
        scratch_shapes=day_scratch,
        out_shape=(shape(*parts), shape(*parts)),
        compiler_params=PARAMS,
        name="days_first",
    )(core, first, signs_t, loadings_t, factor_t, residuals)
    mine, other, _ = sum_firms(send, keep)

    by_day = pl.pallas_call(
        firms_kernel,
        in_specs=inputs(5) + [pl.BlockSpec(memory_space=pl.ANY)],
        scratch_shapes=[
            pltpu.VMEM((days, n), jnp.float32),
            pltpu.VMEM((days, 2 * n), jnp.bfloat16),
            pltpu.VMEM((firms, n), jnp.float32),
            *block_scratch,
        ],
        out_shape=shape(day_ranks, block + factors, n),
        compiler_params=PARAMS,
        name="firms",
    )(core, mine, other, signs, loadings_t, factor_t, residuals)
    raw_loads, _ = turn(lax.all_to_all(by_day, ("x_hi", "y"), 0, 0, tiled=True), block)
    raw_loads = lax.all_to_all(raw_loads, ("x_hi", "y"), 0, 0, tiled=True).reshape(firms, n)

    send, keep = pl.pallas_call(
        days_later_kernel,
        in_specs=inputs(4) + [pl.BlockSpec(memory_space=pl.ANY)],
        scratch_shapes=day_scratch,
        out_shape=(shape(*parts), shape(*parts)),
        compiler_params=PARAMS,
        name="days_later",
    )(core, raw_loads, signs_t, loadings_t, factor_t, residuals)
    mine, other, inverse = sum_firms(send, keep)

    raw_factors, last = pl.pallas_call(
        last_kernel,
        in_specs=inputs(2),
        out_shape=(shape(days, n), shape(day_ranks, factors, n)),
        compiler_params=PARAMS,
        name="last",
    )(core, mine, other)
    last = lax.all_to_all(last, ("x_hi", "y"), 0, 0, tiled=True)
    boot_loadings = pl.pallas_call(
        functools.partial(loadings_kernel, scale=math.sqrt(total_firms)),
        out_shape=shape(firms, n),
        compiler_params=PARAMS,
        name="boot_loadings",
    )(raw_loads, inverse)
    boot_factors = pl.pallas_call(
        functools.partial(factors_kernel, scale=math.sqrt(total_days)),
        out_shape=shape(days, n),
        compiler_params=PARAMS,
        name="boot_factors",
    )(last, raw_factors)
    return boot_loadings, boot_factors


def solution(mesh):
    firm_ranks, day_ranks = mesh.shape["firm"], mesh.shape["day"]
    axes = ("x_lo", "z", "core", "x_hi", "y")
    fine = Mesh(mesh.devices.reshape(2, firm_ranks // 4, 2, 2, day_ranks // 2), axes)
    firm, day = ("x_lo", "z", "core"), ("x_hi", "y")

    def run(residuals, *rest):
        total_firms, total_days = residuals.shape
        body = functools.partial(
            on_device, chips=firm_ranks // 2, total_firms=total_firms, total_days=total_days, day_ranks=day_ranks
        )
        return jax.shard_map(
            body,
            mesh=fine,
            in_specs=(P(firm, day), P(firm, None), P(day, None), P(day, None), P(firm), P()),
            out_specs=(P(firm, None), P(day, None)),
            check_vma=False,
        )(residuals, *rest)

    return run
```

time: 195 us -> 186 us (0.954)
  blocking collectives: 95.2 us -> 108 us
  waiting for transfers between devices: 27.4 us -> 19.2 us
  Pallas kernels: 40.9 us -> 34.5 us
  starting transfers between devices: 27.5 us -> 23.3 us
  local copies, waits for them, and re-layouts: 2.62 us -> 0.01 us
    all_to_all x3 -> x4, blocking collectives: 61 us -> 73.4 us  [the longest x2 46.6 us: sum_firms(): lax.all_to_all(pair, ('x_lo', 'z'), 0, 0, tiled=True)]
    all_to_all x1 -> x0, waiting for transfers between devices: 8.66 us -> none  [on_device(): lax.all_to_all(wide, ('x_hi', 'y'), 0, 0, tiled=True).reshape(firms, n)]
    pallas_call x6 -> x8, Pallas kernels: 37 us -> 30.5 us  [the longest x1 6.78 us: on_device(): pl.pallas_call(first_kernel, in_specs=[pl.BlockSpec(memory_space=pl.ANY)]...]
    all_to_all x1 -> x0, starting transfers between devices: 3.49 us -> none  [on_device(): lax.all_to_all(wide, ('x_hi', 'y'), 0, 0, tiled=True).reshape(firms, n)]
  transfers between devices with their start and end apart: 7 -> 6, of which waited for: 7 -> 6; matrix products, arithmetic and copies ran while one was open for 0% -> 0% of each run, Pallas kernels for 1% -> 1%
where the time goes in v2:
time: 186 us; the launch traced here: 185 us
  blocking collectives  108 us (58%)
  Pallas kernels  34.5 us (19%)
  starting transfers between devices  23.3 us (13%)
  waiting for transfers between devices  19.2 us (10%)
    all_to_all x2, blocking collectives, sum_firms(): lax.all_to_all(pair, ('x_lo', 'z'), 0, 0, tiled=True)  46.6 us
    all_to_all x2, blocking collectives, sum_firms(): lax.all_to_all(mine, ('x_lo', 'z'), 0, 0, tiled=True).reshape(half, n)  34.1 us
    all_to_all x1, blocking collectives, on_device(): lax.all_to_all(by_day, ('x_hi', 'y'), 0, 0, tiled=True)  14.1 us
    all_to_all x1, blocking collectives, on_device(): lax.all_to_all(raw_loads, ('x_hi', 'y'), 0, 0, tiled=True).reshape(firms, n)  12.7 us
    all_to_all x1, waiting for transfers between devices, on_device(): first = lax.all_to_all(first, ('x_hi', 'y'), 0, 0, tiled=True)  7.71 us
    all_to_all x1, starting transfers between devices, on_device(): first = lax.all_to_all(first, ('x_hi', 'y'), 0, 0, tiled=True)  7.49 us
    ppermute x2, starting transfers between devices, sum_firms(): return (mine, lax.ppermute(mine, 'core', [(0, 1), (1, 0)]), inverse)  7.19 us
    pallas_call x1, Pallas kernels, on_device(): pl.pallas_call(first_kernel, in_specs=[pl.BlockSpec(memory_space=pl.ANY)]...  6.78 us
  transfers between devices with their start and end apart: 6, of which 6 were waited for; matrix products, arithmetic and copies ran while one was open for 0% of the time, Pallas kernels for 1%

profile of v2, /device:TPU:1, one launch (start us, length us, event | category | flops | bytes accessed | tf_op | source)
XLA Modules:
  0.0 185.4 jit_solution(5792305805381313989)
XLA Ops:
  0.7 6.8 %first.1 = (f32[8,8,1152]{2,1,0:T(8,128)}, f32[128,1024]{1,0:T(8,128)S(1)}, f32[1024,128]{1,0:T(8,128)S(1)}) custom-call(f32[8,2048]{1,0:T(8,128)} %bitcast.22, f32[8,2048]{1,0:T(8,128)} %bitcast.15, s32[1,1024]{1,0:T(1,128)} %bitcast.24, s32[16,512]{1,0:T(8,128)} %bitcast.23, f32[1024,2048]{1,0:T(8,128)} %res_any.7), custom_call_target="tpu_custom_call" | custom-call | tf_op jit(solution)/shard_map/first/pallas_call | solution.py:276
  7.4 7.5 %all-to-all-start = ((f32[8,8,1152]{2,1,0:T(8,128)}), f32[8,8,1152]{2,1,0:T(8,128)S(1)}, u32[]{:S(2)}, u32[]{:S(2)}) async-start(f32[8,8,1152]{2,1,0:T(8,128)} %get-tuple-element.15), calls=%async_computation | async-start | bytes 589824 | tf_op jit(solution)/shard_map/all_to_all | solution.py:296
  14.9 7.7 %all-to-all-done.got_ref = f32[8,8,1152]{2,1,0:T(8,128)S(1)} async-done(((f32[8,8,1152]{2,1,0:T(8,128)}), f32[8,8,1152]{2,1,0:T(8,128)S(1)}, u32[]{:S(2)}, u32[]{:S(2)}) %all-to-all-start) | async-done | bytes 294944 | tf_op jit(solution)/shard_map/all_to_all | solution.py:296
  22.7 6.0 %days_first.1 = (f32[16,72,128]{2,1,0:T(8,128)S(1)}, f32[16,72,128]{2,1,0:T(8,128)S(1)}) custom-call(s32[1]{0:T(128)} %bitcast.core_ref, f32[8,8,1152]{2,1,0:T(8,128)S(1)} %all-to-all-done.got_ref, f32[128,1024]{1,0:T(8,128)S(1)} %get-tuple-element.16.signs_ref, f32[8,1024]{1,0:T(8,128)S(1)} %bitcast.19, f32[8,2048]{1,0:T(8,128)S(1)} %bitcast.16, ...), custom_call_target="tpu_custom_call" | custom-call | tf_op jit(solution)/shard_map/days_first/pallas_call | solution.py:315
  28.7 2.4 %collective-permute-start = (f32[16,72,128]{2,1,0:T(8,128)S(1)}, f32[16,72,128]{2,1,0:T(8,128)S(1)}, u32[]{:S(2)}, u32[]{:S(2)}) collective-permute-start(f32[16,72,128]{2,1,0:T(8,128)S(1)} %get-tuple-element.18), channel_id=1, source_target_pairs={{0,8},{8,0},{1,9},{9,1},{2,10},{10,2},{3,11},{11,3},{4,12},{12,4},... | collective-permute-start | bytes 1769480 | tf_op jit(solution)/shard_map/ppermute | solution.py:310
  31.0 1.6 collective-permute-done
  32.7 25.4 %all_to_all.40.got_ref = f32[16,72,128]{2,1,0:T(8,128)S(1)} all-to-all(f32[16,72,128]{2,1,0:T(8,128)S(1)} %add.6), channel_id=1, replica_groups=mesh['x_lo'=2,'z'=8,'core'=2,'x_hi'=2,'y'=4] {'x_lo','z'}, dimensions={0} | all-to-all | bytes 1179648 | tf_op jit(solution)/shard_map/all_to_all | solution.py:311
  59.4 17.1 %all_to_all.41 = f32[16,64,128]{2,1,0:T(8,128)S(1)} all-to-all(f32[16,64,128]{2,1,0:T(8,128)S(1)} %get-tuple-element.19), channel_id=1, replica_groups=mesh['x_lo'=2,'z'=8,'core'=2,'x_hi'=2,'y'=4] {'x_lo','z'}, dimensions={0} | all-to-all | bytes 1048576 | tf_op jit(solution)/shard_map/all_to_all | solution.py:312
  76.5 3.6 %collective-permute-start.1 = (f32[1024,128]{1,0:T(8,128)S(1)}, f32[1024,128]{1,0:T(8,128)S(1)}, u32[]{:S(2)}, u32[]{:S(2)}) collective-permute-start(f32[1024,128]{1,0:T(8,128)S(1)} %bitcast.13), channel_id=1, source_target_pairs={{0,8},{8,0},{1,9},{9,1},{2,10},{10,2},{3,11},{11,3},{4,12},{12,4},... | collective-permute-start | bytes 1572872 | tf_op jit(solution)/shard_map/ppermute | solution.py:313
  80.1 1.5 collective-permute-done.1.other_ref
  81.7 6.4 %firms.1 = f32[8,136,128]{2,1,0:T(8,128)S(1)} custom-call(s32[1]{0:T(128)} %bitcast.core_ref, f32[1024,128]{1,0:T(8,128)S(1)} %bitcast.14, f32[1024,128]{1,0:T(8,128)S(1)} %collective-permute-done.1.other_ref, f32[1024,128]{1,0:T(8,128)S(1)} %get-tuple-element.20.signs_ref, f32[8,1024]{1,0:T(8,128)S(1)} %bitcast.20, f32[8,2048]{1,0:T(8,128)S(1)} %bitcast.17, ...), custom_call_target="tpu_custom_call" | custom-call | tf_op jit(solution)/shard_map/firms/pallas_call | solution.py:325
  88.1 14.1 %all_to_all.42.got_ref = f32[8,136,128]{2,1,0:T(8,128)S(1)} all-to-all(f32[8,136,128]{2,1,0:T(8,128)S(1)} %firms.1), channel_id=1, replica_groups=mesh['x_lo'=2,'z'=8,'core'=2,'x_hi'=2,'y'=4] {'x_hi','y'}, dimensions={0} | all-to-all | bytes 1114112 | tf_op jit(solution)/shard_map/all_to_all | solution.py:338
  103.5 12.7 %all_to_all.43 = f32[8,128,128]{2,1,0:T(8,128)S(1)} all-to-all(f32[8,128,128]{2,1,0:T(8,128)S(1)} %get-tuple-element.21), channel_id=1, replica_groups=mesh['x_lo'=2,'z'=8,'core'=2,'x_hi'=2,'y'=4] {'x_hi','y'}, dimensions={0} | all-to-all | bytes 1048576 | tf_op jit(solution)/shard_map/all_to_all | solution.py:339
  116.2 6.0 %days_later.1 = (f32[16,72,128]{2,1,0:T(8,128)S(1)}, f32[16,72,128]{2,1,0:T(8,128)S(1)}) custom-call(s32[1]{0:T(128)} %bitcast.core_ref, f32[1024,128]{1,0:T(8,128)S(1)} %bitcast.9, f32[128,1024]{1,0:T(8,128)S(1)} %get-tuple-element.16.signs_ref, f32[8,1024]{1,0:T(8,128)S(1)} %bitcast.21, f32[8,2048]{1,0:T(8,128)S(1)} %bitcast.18, f32[1024,2048]{1,0:T(8,128)} %res_any.7), custom_call_target="tpu_custom_call" | custom-call | tf_op jit(solution)/shard_map/days_later/pallas_call | solution.py:341
  122.2 2.9 %collective-permute-start.2 = (f32[16,72,128]{2,1,0:T(8,128)S(1)}, f32[16,72,128]{2,1,0:T(8,128)S(1)}, u32[]{:S(2)}, u32[]{:S(2)}) collective-permute-start(f32[16,72,128]{2,1,0:T(8,128)S(1)} %get-tuple-element.23), channel_id=1, source_target_pairs={{0,8},{8,0},{1,9},{9,1},{2,10},{10,2},{3,11},{11,3},{4,12},{12,4},... | collective-permute-start | bytes 1769480 | tf_op jit(solution)/shard_map/ppermute | solution.py:310
  125.1 1.6 collective-permute-done.2
  126.8 21.2 %all_to_all.44.got_ref = f32[16,72,128]{2,1,0:T(8,128)S(1)} all-to-all(f32[16,72,128]{2,1,0:T(8,128)S(1)} %add.7), channel_id=1, replica_groups=mesh['x_lo'=2,'z'=8,'core'=2,'x_hi'=2,'y'=4] {'x_lo','z'}, dimensions={0} | all-to-all | bytes 1179648 | tf_op jit(solution)/shard_map/all_to_all | solution.py:311
  148.9 17.1 %all_to_all.45 = f32[16,64,128]{2,1,0:T(8,128)S(1)} all-to-all(f32[16,64,128]{2,1,0:T(8,128)S(1)} %get-tuple-element.25), channel_id=1, replica_groups=mesh['x_lo'=2,'z'=8,'core'=2,'x_hi'=2,'y'=4] {'x_lo','z'}, dimensions={0} | all-to-all | bytes 1048576 | tf_op jit(solution)/shard_map/all_to_all | solution.py:312
  166.0 3.6 %collective-permute-start.3 = (f32[1024,128]{1,0:T(8,128)S(1)}, f32[1024,128]{1,0:T(8,128)S(1)}, u32[]{:S(2)}, u32[]{:S(2)}) collective-permute-start(f32[1024,128]{1,0:T(8,128)S(1)} %bitcast.11), channel_id=1, source_target_pairs={{0,8},{8,0},{1,9},{9,1},{2,10},{10,2},{3,11},{11,3},{4,12},{12,4},... | collective-permute-start | bytes 1572872 | tf_op jit(solution)/shard_map/ppermute | solution.py:313
  169.6 1.5 collective-permute-done.3.other_ref
  171.1 1.8 last.1
  172.9 3.3 %all-to-all-start.7 = ((f32[8,8,128]{2,1,0:T(8,128)}), f32[8,8,128]{2,1,0:T(8,128)S(1)}, u32[]{:S(2)}, u32[]{:S(2)}) async-start(f32[8,8,128]{2,1,0:T(8,128)} %get-tuple-element.26), calls=%async_computation.7 | async-start | bytes 65536 | tf_op jit(solution)/shard_map/all_to_all | solution.py:358
  177.6 5.2 %all-to-all-done.7.got_ref = f32[8,8,128]{2,1,0:T(8,128)S(1)} async-done(((f32[8,8,128]{2,1,0:T(8,128)}), f32[8,8,128]{2,1,0:T(8,128)S(1)}, u32[]{:S(2)}, u32[]{:S(2)}) %all-to-all-start.7) | async-done | bytes 32800 | tf_op jit(solution)/shard_map/all_to_all | solution.py:358
  182.8 2.6 %boot_factors.1 = f32[2048,128]{1,0:T(8,128)} custom-call(f32[8,8,128]{2,1,0:T(8,128)S(1)} %all-to-all-done.7.got_ref, f32[2048,128]{1,0:T(8,128)S(1)} %get-tuple-element.27.raw_ref), custom_call_target="tpu_custom_call" | custom-call | tf_op jit(solution)/shard_map/boot_factors/pallas_call | solution.py:365
  (10 shorter events, 5.0 us)
Async XLA Ops:
  0.6 22.0 %copy-start = (f32[2048,8]{0,1:T(8,128)S(1)}, f32[2048,8]{0,1:T(8,128)}, u32[]{:S(2)}) copy-start(f32[2048,8]{0,1:T(8,128)} %param.8) | copy-start | bytes 196612
  0.6 22.0 %copy-start.1 = (f32[1024,8]{0,1:T(8,128)S(1)}, f32[1024,8]{0,1:T(8,128)}, u32[]{:S(2)}) copy-start(f32[1024,8]{0,1:T(8,128)} %param.7) | copy-start | bytes 98308
  7.4 15.2 %all-to-all-start = ((f32[8,8,1152]{2,1,0:T(8,128)}), f32[8,8,1152]{2,1,0:T(8,128)S(1)}, u32[]{:S(2)}, u32[]{:S(2)}) async-start(f32[8,8,1152]{2,1,0:T(8,128)} %get-tuple-element.15), calls=%async_computation | async-start | bytes 589824 | tf_op jit(solution)/shard_map/all_to_all | solution.py:296
  28.7 4.0 %collective-permute-start = (f32[16,72,128]{2,1,0:T(8,128)S(1)}, f32[16,72,128]{2,1,0:T(8,128)S(1)}, u32[]{:S(2)}, u32[]{:S(2)}) collective-permute-start(f32[16,72,128]{2,1,0:T(8,128)S(1)} %get-tuple-element.18), channel_id=1, source_target_pairs={{0,8},{8,0},{1,9},{9,1},{2,10},{10,2},{3,11},{11,3},{4,12},{12,4},... | collective-permute-start | bytes 1769480 | tf_op jit(solution)/shard_map/ppermute | solution.py:310
  76.5 5.1 %collective-permute-start.1 = (f32[1024,128]{1,0:T(8,128)S(1)}, f32[1024,128]{1,0:T(8,128)S(1)}, u32[]{:S(2)}, u32[]{:S(2)}) collective-permute-start(f32[1024,128]{1,0:T(8,128)S(1)} %bitcast.13), channel_id=1, source_target_pairs={{0,8},{8,0},{1,9},{9,1},{2,10},{10,2},{3,11},{11,3},{4,12},{12,4},... | collective-permute-start | bytes 1572872 | tf_op jit(solution)/shard_map/ppermute | solution.py:313
  122.2 4.6 %collective-permute-start.2 = (f32[16,72,128]{2,1,0:T(8,128)S(1)}, f32[16,72,128]{2,1,0:T(8,128)S(1)}, u32[]{:S(2)}, u32[]{:S(2)}) collective-permute-start(f32[16,72,128]{2,1,0:T(8,128)S(1)} %get-tuple-element.23), channel_id=1, source_target_pairs={{0,8},{8,0},{1,9},{9,1},{2,10},{10,2},{3,11},{11,3},{4,12},{12,4},... | collective-permute-start | bytes 1769480 | tf_op jit(solution)/shard_map/ppermute | solution.py:310
  166.0 5.1 %collective-permute-start.3 = (f32[1024,128]{1,0:T(8,128)S(1)}, f32[1024,128]{1,0:T(8,128)S(1)}, u32[]{:S(2)}, u32[]{:S(2)}) collective-permute-start(f32[1024,128]{1,0:T(8,128)S(1)} %bitcast.11), channel_id=1, source_target_pairs={{0,8},{8,0},{1,9},{9,1},{2,10},{10,2},{3,11},{11,3},{4,12},{12,4},... | collective-permute-start | bytes 1572872 | tf_op jit(solution)/shard_map/ppermute | solution.py:313
  172.9 9.9 %all-to-all-start.7 = ((f32[8,8,128]{2,1,0:T(8,128)}), f32[8,8,128]{2,1,0:T(8,128)S(1)}, u32[]{:S(2)}, u32[]{:S(2)}) async-start(f32[8,8,128]{2,1,0:T(8,128)} %get-tuple-element.26), calls=%async_computation.7 | async-start | bytes 65536 | tf_op jit(solution)/shard_map/all_to_all | solution.py:358

commit v3 on v2

--- a/solution.py
+++ b/solution.py
@@ -10,7 +10,8 @@
 from jax.sharding import PartitionSpec as P
 
 STEPS = 4
-AHEAD = 4
+PIECES = 2
+AHEAD = 8
 HIGHEST = lax.Precision.HIGHEST
 NN = (((1,), (0,)), ((), ()))
 NT = (((1,), (1,)), ((), ()))
@@ -29,6 +30,41 @@
 def split(x):
     high = x.astype(jnp.bfloat16)
     return high, (x - high.astype(jnp.float32)).astype(jnp.bfloat16)
+
+
+def split3(x):
+    high = x.astype(jnp.bfloat16)
+    rest = x - high.astype(jnp.float32)
+    middle = rest.astype(jnp.bfloat16)
+    return high, middle, (rest - middle.astype(jnp.float32)).astype(jnp.bfloat16)
+
+
+def corners(both, rows, cols):
+    return both[:rows, :cols] + (both[:rows, cols:] + both[rows:, :cols] + both[rows:, cols:])
+
+
+def gram_of(high, middle, low, dims, axis):
+    both = jnp.concatenate([high, middle], axis=axis)
+    n = both.shape[axis] // 2
+    cross = fast(high, low, dims)
+    return corners(fast(both, both, dims), n, n) + (cross + cross.T)
+
+
+def stack(x, order):
+    high = x.astype(jnp.bfloat16).astype(jnp.float32)
+    parts = {"h": high, "l": x - high, "0": jnp.zeros_like(x)}
+    return jnp.concatenate([parts[p] for p in order], axis=0).astype(jnp.bfloat16)
+
+
+def rotated(x, inverse):
+    n = inverse.shape[0]
+    high, low = split(x)
+    top, rest = split(inverse.T)
+    right = jnp.concatenate(
+        [jnp.concatenate([top, rest], axis=1), jnp.concatenate([top, jnp.zeros_like(rest)], axis=1)], axis=0
+    )
+    both = fast(jnp.concatenate([high, low], axis=1), right, NN)
+    return both[:, 0:n] + both[:, n:]
 
 
 def compact(full, factors):
@@ -80,17 +116,33 @@
     return (slice(t * rows, (t + 1) * rows), slice(None))
 
 
-def bring(res_any, res_ref, sems, tiles):
-    copies = [pltpu.make_async_copy(res_any.at[tile], res_ref.at[tile], sems.at[t]) for t, tile in enumerate(tiles)]
+def bring(pairs, sems):
+    copies = [pltpu.make_async_copy(a, b, sems.at[t]) for t, (a, b) in enumerate(pairs)]
     for copy in copies[:AHEAD]:
         copy.start()
     return copies
 
 
 def arrive(copies, t):
-    copies[t].wait()
-    if t + AHEAD < len(copies):
-        copies[t + AHEAD].start()
+    for p in range(t * PIECES, (t + 1) * PIECES):
+        copies[p].wait()
+        if p + AHEAD < len(copies):
+            copies[p + AHEAD].start()
+
+
+def piece_pairs(res_any, res_ref, piece):
+    size = res_ref.shape[1] if piece is columns else res_ref.shape[0]
+    count = STEPS * PIECES
+    return [(res_any.at[piece(p, size // count)], res_ref.at[piece(p, size // count)]) for p in range(count)]
+
+
+def bring_for_core(core, res_any, res_ref, sems):
+    days = res_ref.shape[1]
+    count = STEPS * PIECES
+    width = days // count
+    firsts = [pl.multiple_of(((1 - core) if p < count // 2 else core) * (days // 2) + p % (count // 2) * width, width) for p in range(count)]
+    pairs = [(res_any.at[:, pl.ds(firsts[p], width)], res_ref.at[columns(p, width)]) for p in range(count)]
+    return bring(pairs, sems), firsts[::PIECES]
 
 
 def first_kernel(
@@ -102,18 +154,18 @@
     firms, days = res_ref.shape
     n = total_ref.shape[1]
     pairs = [(start_any, start_ref), (factor_any, factor_ref), (ids_any, ids_ref), (bits_any, bits_ref)]
-    small = [pltpu.make_async_copy(a, b, sems.at[STEPS + i]) for i, (a, b) in enumerate(pairs)]
+    small = [pltpu.make_async_copy(a, b, sems.at[STEPS * PIECES + i]) for i, (a, b) in enumerate(pairs)]
     for copy in small:
         copy.start()
     tiles = [columns(t, days // STEPS) for t in range(STEPS)]
-    large = bring(res_any, res_ref, sems, tiles)
+    large = bring(piece_pairs(res_any, res_ref, columns), sems)
     for copy in small:
         copy.wait()
     start = start_ref[...]
     high = start.astype(jnp.bfloat16).astype(jnp.float32)
     both = jnp.concatenate([high, start - high, jnp.zeros((n - 2 * factors, days), jnp.float32)], axis=0)
     both = both.T.astype(jnp.bfloat16)
-    mixed = exact(start, factor_ref[...], NT)
+    mixed = corners(fast(stack(start, "hl"), stack(factor_ref[...], "hl"), NT), factors, factors)
     mixed = jnp.concatenate([mixed, jnp.zeros((factors, width - firms - factors), jnp.float32)], axis=1)
     out_ref[:, :, firms:] = jnp.broadcast_to(mixed[None], (copies, factors, width - firms))
     put_signs(ids_ref, bits_ref, wide_ref, tall_ref)
@@ -128,36 +180,34 @@
     out_ref[:, :, 0:firms] = jnp.broadcast_to(total[None], (copies, factors, firms))
 
 
-def days_from(raw_t, signs_ref, loadings_ref, left_ref, small_ref):
+def days_from(raw_t, signs_ref, loadings_ref, factor_ref, left_ref, small_ref, right_ref):
     factors = loadings_ref.shape[0]
     n = raw_t.shape[0]
-    high, low = split(signs_ref[...] * raw_t)
-    left_ref[0:n] = high
-    left_ref[n:] = low
-    small_ref[...] = exact(raw_t, loadings_ref[...], NT)
-    return compact(exact(raw_t, raw_t, NT), factors)
-
-
-def days_tiles(core, copies, tiles, factor_ref, res_ref, left_ref, small_ref, send_ref, keep_ref):
-    n = small_ref.shape[0]
-    rows = send_ref.shape[1] - factor_ref.shape[0]
+    high, middle, low = split3(raw_t)
+    signs = signs_ref[...]
+    left_ref[0:n] = (signs * high.astype(jnp.float32)).astype(jnp.bfloat16)
+    left_ref[n:] = (signs * middle.astype(jnp.float32)).astype(jnp.bfloat16)
+    both = jnp.concatenate([high, middle], axis=0)
+    small = corners(fast(stack(loadings_ref[...], "hl"), both, NT), factors, n)
+    small_ref[...] = stack(small, "hhl0")
+    right_ref[...] = stack(factor_ref[...], "hlh0")
+    return compact(gram_of(high, middle, low, NT, 0), factors)
+
+
+def days_tiles(copies, firsts, res_ref, left_ref, small_ref, right_ref, send_ref, keep_ref):
+    n = small_ref.shape[1]
+    rows = send_ref.shape[1] - small_ref.shape[0] // 4
     width = res_ref.shape[1] // STEPS
     half = STEPS // 2
     for t in range(STEPS):
         arrive(copies, t)
-        high, low = split(res_ref[tiles[t]])
+        high, low = split(res_ref[columns(t, width)])
         both = fast(left_ref[...], high, NN)
-        tile = both[0:n] + both[n:] + fast(left_ref[0:n], low, NN) + exact(small_ref[...], factor_ref[tiles[t]], NN)
-        tile = tile.T.reshape(width // rows, rows, n)
+        more = fast(small_ref[...], right_ref[:, pl.ds(firsts[t], width)], TN)
+        tile = both[0:n] + both[n:] + fast(left_ref[0:n], low, NN) + more
+        out_ref = send_ref if t < half else keep_ref
         at = slice(t % half * (width // rows), (t % half + 1) * (width // rows))
-
-        @pl.when(core != t // half)
-        def _():
-            send_ref[at, 0:rows, :] = tile
-
-        @pl.when(core == t // half)
-        def _():
-            keep_ref[at, 0:rows, :] = tile
+        out_ref[at, 0:rows, :] = tile.T.reshape(width // rows, rows, n)
 
 
 def put_gram(gram, send_ref, keep_ref):
@@ -167,9 +217,8 @@
     keep_ref[:, rows - gram.shape[0] :, :] = wide
 
 
-def days_first_kernel(core_ref, got_ref, signs_ref, loadings_ref, factor_ref, res_any, send_ref, keep_ref, left_ref, small_ref, res_ref, sems):
-    tiles = [columns(t, res_ref.shape[1] // STEPS) for t in range(STEPS)]
-    copies = bring(res_any, res_ref, sems, tiles)
+def days_first_kernel(core_ref, got_ref, signs_ref, loadings_ref, factor_ref, res_any, send_ref, keep_ref, left_ref, small_ref, right_ref, res_ref, sems):
+    copies, firsts = bring_for_core(core_ref[0], res_any, res_ref, sems)
     factors, firms = loadings_ref.shape
     n = signs_ref.shape[0]
     got = got_ref[...].sum(axis=0)
@@ -180,34 +229,33 @@
     reps = n // factors
     raw_t = signs_ref[...] * jnp.concatenate([by_residuals] * reps, axis=0)
     raw_t = raw_t + jnp.concatenate([by_factors] * reps, axis=0)
-    put_gram(days_from(raw_t, signs_ref, loadings_ref, left_ref, small_ref), send_ref, keep_ref)
-    days_tiles(core_ref[0], copies, tiles, factor_ref, res_ref, left_ref, small_ref, send_ref, keep_ref)
-
-
-def days_later_kernel(core_ref, got_ref, signs_ref, loadings_ref, factor_ref, res_any, send_ref, keep_ref, left_ref, small_ref, res_ref, sems):
-    tiles = [columns(t, res_ref.shape[1] // STEPS) for t in range(STEPS)]
-    copies = bring(res_any, res_ref, sems, tiles)
-    put_gram(days_from(got_ref[...].T, signs_ref, loadings_ref, left_ref, small_ref), send_ref, keep_ref)
-    days_tiles(core_ref[0], copies, tiles, factor_ref, res_ref, left_ref, small_ref, send_ref, keep_ref)
+    put_gram(days_from(raw_t, signs_ref, loadings_ref, factor_ref, left_ref, small_ref, right_ref), send_ref, keep_ref)
+    days_tiles(copies, firsts, res_ref, left_ref, small_ref, right_ref, send_ref, keep_ref)
+
+
+def days_later_kernel(core_ref, got_ref, signs_ref, loadings_ref, factor_ref, res_any, send_ref, keep_ref, left_ref, small_ref, right_ref, res_ref, sems):
+    copies, firsts = bring_for_core(core_ref[0], res_any, res_ref, sems)
+    put_gram(days_from(got_ref[...].T, signs_ref, loadings_ref, factor_ref, left_ref, small_ref, right_ref), send_ref, keep_ref)
+    days_tiles(copies, firsts, res_ref, left_ref, small_ref, right_ref, send_ref, keep_ref)
 
 
 def firms_kernel(core_ref, mine_ref, other_ref, signs_ref, loadings_ref, factor_ref, res_any, out_ref, raw_ref, right_ref, add_ref, res_ref, sems):
     factors = loadings_ref.shape[0]
     half, n = mine_ref.shape
     rows = res_ref.shape[0] // STEPS
-    tiles = [rows_of(t, rows) for t in range(STEPS)]
-    large = bring(res_any, res_ref, sems, tiles)
+    large = bring(piece_pairs(res_any, res_ref, rows_of), sems)
     core = core_ref[0]
     raw_ref[pl.ds(pl.multiple_of(core * half, half), half), :] = mine_ref[...]
     raw_ref[pl.ds(pl.multiple_of((1 - core) * half, half), half), :] = other_ref[...]
     raw = raw_ref[...]
-    high, low = split(raw)
+    high, middle, low = split3(raw)
     right_ref[:, 0:n] = high
-    right_ref[:, n:] = low
-    gram = compact(exact(raw, raw, TN), factors)
+    right_ref[:, n:] = middle
+    gram = compact(gram_of(high, middle, low, TN, 1), factors)
     copies, total = out_ref.shape[0], out_ref.shape[1]
     out_ref[:, total - factors :, :] = jnp.broadcast_to(gram[None], (copies, factors, n))
-    add_ref[...] = exact(loadings_ref[...], exact(factor_ref[...], raw, NN), TN)
+    small = corners(fast(stack(factor_ref[...], "hl"), right_ref[...], NN), factors, n)
+    add_ref[...] = fast(stack(loadings_ref[...], "hlh0"), stack(small, "hhl0"), TN)
     block = total - factors
     for t in range(STEPS):
         arrive(large, t)
@@ -234,17 +282,17 @@
     core = core_ref[0]
     raw_ref[pl.ds(pl.multiple_of(core * half, half), half), :] = mine
     raw_ref[pl.ds(pl.multiple_of((1 - core) * half, half), half), :] = other
-    gram = compact(exact(mine, mine, TN) + exact(other, other, TN), out_ref.shape[1])
+    gram = compact(gram_of(*split3(mine), TN, 1) + gram_of(*split3(other), TN, 1), out_ref.shape[1])
     out_ref[...] = jnp.broadcast_to(gram[None], out_ref.shape)
 
 
 def loadings_kernel(raw_ref, inverse_ref, out_ref, *, scale):
-    out_ref[...] = scale * exact(raw_ref[...], inverse_ref[...], NT)
+    out_ref[...] = rotated(raw_ref[...], scale * inverse_ref[...])
 
 
 def factors_kernel(got_ref, raw_ref, out_ref, *, scale):
     gram = got_ref[...].sum(axis=0)
-    out_ref[...] = scale * exact(raw_ref[...], inverse_blocks(gram, gram.shape[0]), NT)
+    out_ref[...] = rotated(raw_ref[...], scale * inverse_blocks(gram, gram.shape[0]))
 
 
 def shape(*dims):
@@ -272,7 +320,7 @@
     core = lax.axis_index("core").astype(jnp.int32).reshape(1)
 
     residuals = in_hbm(residuals)
-    block_scratch = [pltpu.VMEM((firms, days), jnp.float32), pltpu.SemaphoreType.DMA((STEPS,))]
+    block_scratch = [pltpu.VMEM((firms, days), jnp.float32), pltpu.SemaphoreType.DMA((STEPS * PIECES,))]
     first, signs_t, signs = pl.pallas_call(
         first_kernel,
         in_specs=[pl.BlockSpec(memory_space=pl.ANY)] * 5,
@@ -288,14 +336,19 @@
             pltpu.VMEM((reps, clusters), jnp.int32),
             pltpu.VMEM((firms, days), jnp.float32),
             pltpu.VMEM((firms, n), jnp.float32),
-            pltpu.SemaphoreType.DMA((STEPS + 4,)),
+            pltpu.SemaphoreType.DMA((STEPS * PIECES + 4,)),
         ],
         compiler_params=PARAMS,
         name="first",
     )(in_hbm(start_t), in_hbm(factor_t), in_hbm(cluster_ids.reshape(1, firms)), in_hbm(sign_bits.T), residuals)
     first = lax.all_to_all(first, ("x_hi", "y"), 0, 0, tiled=True)
 
-    day_scratch = [pltpu.VMEM((2 * n, firms), jnp.bfloat16), pltpu.VMEM((n, factors), jnp.float32), *block_scratch]
+    day_scratch = [
+        pltpu.VMEM((2 * n, firms), jnp.bfloat16),
+        pltpu.VMEM((4 * factors, n), jnp.bfloat16),
+        pltpu.VMEM((4 * factors, days), jnp.bfloat16),
+        *block_scratch,
+    ]
     parts = (chips, chunk + factors, n)
 
     def turn(got, rows):

time: 186 us -> 181 us (0.973)
  Pallas kernels: 34.5 us -> 29.6 us
where the time goes in v3:
time: 181 us
  blocking collectives  108 us (60%)
  Pallas kernels  29.6 us (16%)
  starting transfers between devices  23.3 us (13%)
  waiting for transfers between devices  19.4 us (11%)
    all_to_all x2, blocking collectives, sum_firms(): lax.all_to_all(pair, ('x_lo', 'z'), 0, 0, tiled=True)  46.7 us
    all_to_all x2, blocking collectives, sum_firms(): lax.all_to_all(mine, ('x_lo', 'z'), 0, 0, tiled=True).reshape(half, n)  34.1 us
    all_to_all x1, blocking collectives, on_device(): lax.all_to_all(by_day, ('x_hi', 'y'), 0, 0, tiled=True)  14.5 us
    all_to_all x1, blocking collectives, on_device(): lax.all_to_all(raw_loads, ('x_hi', 'y'), 0, 0, tiled=True).reshape(firms, n)  12.4 us
    all_to_all x1, waiting for transfers between devices, on_device(): first = lax.all_to_all(first, ('x_hi', 'y'), 0, 0, tiled=True)  7.71 us
    all_to_all x1, starting transfers between devices, on_device(): first = lax.all_to_all(first, ('x_hi', 'y'), 0, 0, tiled=True)  7.49 us
    ppermute x2, starting transfers between devices, sum_firms(): return (mine, lax.ppermute(mine, 'core', [(0, 1), (1, 0)]), inverse)  7.19 us
    pallas_call x1, Pallas kernels, on_device(): pl.pallas_call(first_kernel, in_specs=[pl.BlockSpec(memory_space=pl.ANY)]...  6.73 us
  transfers between devices with their start and end apart: 6, of which 6 were waited for; matrix products, arithmetic and copies ran while one was open for 0% of the time, Pallas kernels for 1%

profile of v3, /device:TPU:1, one launch (start us, length us, event | category | flops | bytes accessed | tf_op | source)
XLA Modules:
  0.0 180.9 jit_solution(15964620852498189962)
XLA Ops:
  0.7 6.7 %first.1 = (f32[8,8,1152]{2,1,0:T(8,128)}, f32[128,1024]{1,0:T(8,128)S(1)}, f32[1024,128]{1,0:T(8,128)S(1)}) custom-call(f32[8,2048]{1,0:T(8,128)} %bitcast.22, f32[8,2048]{1,0:T(8,128)} %bitcast.15, s32[1,1024]{1,0:T(1,128)} %bitcast.24, s32[16,512]{1,0:T(8,128)} %bitcast.23, f32[1024,2048]{1,0:T(8,128)} %res_any.7), custom_call_target="tpu_custom_call" | custom-call | tf_op jit(solution)/shard_map/first/pallas_call | solution.py:324
  7.4 7.5 %all-to-all-start = ((f32[8,8,1152]{2,1,0:T(8,128)}), f32[8,8,1152]{2,1,0:T(8,128)S(1)}, u32[]{:S(2)}, u32[]{:S(2)}) async-start(f32[8,8,1152]{2,1,0:T(8,128)} %get-tuple-element.15), calls=%async_computation | async-start | bytes 589824 | tf_op jit(solution)/shard_map/all_to_all | solution.py:344
  14.9 7.7 %all-to-all-done.got_ref = f32[8,8,1152]{2,1,0:T(8,128)S(1)} async-done(((f32[8,8,1152]{2,1,0:T(8,128)}), f32[8,8,1152]{2,1,0:T(8,128)S(1)}, u32[]{:S(2)}, u32[]{:S(2)}) %all-to-all-start) | async-done | bytes 294944 | tf_op jit(solution)/shard_map/all_to_all | solution.py:344
  22.6 4.8 %days_first.1 = (f32[16,72,128]{2,1,0:T(8,128)S(1)}, f32[16,72,128]{2,1,0:T(8,128)S(1)}) custom-call(s32[1]{0:T(128)} %bitcast.core_ref, f32[8,8,1152]{2,1,0:T(8,128)S(1)} %all-to-all-done.got_ref, f32[128,1024]{1,0:T(8,128)S(1)} %get-tuple-element.16.signs_ref, f32[8,1024]{1,0:T(8,128)S(1)} %bitcast.19, f32[8,2048]{1,0:T(8,128)S(1)} %bitcast.16, ...), custom_call_target="tpu_custom_call" | custom-call | tf_op jit(solution)/shard_map/days_first/pallas_call | solution.py:368
  27.4 2.4 %collective-permute-start = (f32[16,72,128]{2,1,0:T(8,128)S(1)}, f32[16,72,128]{2,1,0:T(8,128)S(1)}, u32[]{:S(2)}, u32[]{:S(2)}) collective-permute-start(f32[16,72,128]{2,1,0:T(8,128)S(1)} %get-tuple-element.18), channel_id=1, source_target_pairs={{0,8},{8,0},{1,9},{9,1},{2,10},{10,2},{3,11},{11,3},{4,12},{12,4},... | collective-permute-start | bytes 1769480 | tf_op jit(solution)/shard_map/ppermute | solution.py:363
  29.7 1.6 collective-permute-done
  31.4 25.4 %all_to_all.40.got_ref = f32[16,72,128]{2,1,0:T(8,128)S(1)} all-to-all(f32[16,72,128]{2,1,0:T(8,128)S(1)} %add.6), channel_id=1, replica_groups=mesh['x_lo'=2,'z'=8,'core'=2,'x_hi'=2,'y'=4] {'x_lo','z'}, dimensions={0} | all-to-all | bytes 1179648 | tf_op jit(solution)/shard_map/all_to_all | solution.py:364
  58.1 17.1 %all_to_all.41 = f32[16,64,128]{2,1,0:T(8,128)S(1)} all-to-all(f32[16,64,128]{2,1,0:T(8,128)S(1)} %get-tuple-element.19), channel_id=1, replica_groups=mesh['x_lo'=2,'z'=8,'core'=2,'x_hi'=2,'y'=4] {'x_lo','z'}, dimensions={0} | all-to-all | bytes 1048576 | tf_op jit(solution)/shard_map/all_to_all | solution.py:365
  75.2 3.6 %collective-permute-start.1 = (f32[1024,128]{1,0:T(8,128)S(1)}, f32[1024,128]{1,0:T(8,128)S(1)}, u32[]{:S(2)}, u32[]{:S(2)}) collective-permute-start(f32[1024,128]{1,0:T(8,128)S(1)} %bitcast.13), channel_id=1, source_target_pairs={{0,8},{8,0},{1,9},{9,1},{2,10},{10,2},{3,11},{11,3},{4,12},{12,4},... | collective-permute-start | bytes 1572872 | tf_op jit(solution)/shard_map/ppermute | solution.py:366
  78.8 1.5 collective-permute-done.1.other_ref
  80.3 5.3 %firms.1 = f32[8,136,128]{2,1,0:T(8,128)S(1)} custom-call(s32[1]{0:T(128)} %bitcast.core_ref, f32[1024,128]{1,0:T(8,128)S(1)} %bitcast.14, f32[1024,128]{1,0:T(8,128)S(1)} %collective-permute-done.1.other_ref, f32[1024,128]{1,0:T(8,128)S(1)} %get-tuple-element.20.signs_ref, f32[8,1024]{1,0:T(8,128)S(1)} %bitcast.20, f32[8,2048]{1,0:T(8,128)S(1)} %bitcast.17, ...), custom_call_target="tpu_custom_call" | custom-call | tf_op jit(solution)/shard_map/firms/pallas_call | solution.py:378
  85.6 14.5 %all_to_all.42.got_ref = f32[8,136,128]{2,1,0:T(8,128)S(1)} all-to-all(f32[8,136,128]{2,1,0:T(8,128)S(1)} %firms.1), channel_id=1, replica_groups=mesh['x_lo'=2,'z'=8,'core'=2,'x_hi'=2,'y'=4] {'x_hi','y'}, dimensions={0} | all-to-all | bytes 1114112 | tf_op jit(solution)/shard_map/all_to_all | solution.py:391
  101.4 12.4 %all_to_all.43 = f32[8,128,128]{2,1,0:T(8,128)S(1)} all-to-all(f32[8,128,128]{2,1,0:T(8,128)S(1)} %get-tuple-element.21), channel_id=1, replica_groups=mesh['x_lo'=2,'z'=8,'core'=2,'x_hi'=2,'y'=4] {'x_hi','y'}, dimensions={0} | all-to-all | bytes 1048576 | tf_op jit(solution)/shard_map/all_to_all | solution.py:392
  113.8 4.7 %days_later.1 = (f32[16,72,128]{2,1,0:T(8,128)S(1)}, f32[16,72,128]{2,1,0:T(8,128)S(1)}) custom-call(s32[1]{0:T(128)} %bitcast.core_ref, f32[1024,128]{1,0:T(8,128)S(1)} %bitcast.9, f32[128,1024]{1,0:T(8,128)S(1)} %get-tuple-element.16.signs_ref, f32[8,1024]{1,0:T(8,128)S(1)} %bitcast.21, f32[8,2048]{1,0:T(8,128)S(1)} %bitcast.18, f32[1024,2048]{1,0:T(8,128)} %res_any.7), custom_call_target="tpu_custom_call" | custom-call | tf_op jit(solution)/shard_map/days_later/pallas_call | solution.py:394
  118.4 2.9 %collective-permute-start.2 = (f32[16,72,128]{2,1,0:T(8,128)S(1)}, f32[16,72,128]{2,1,0:T(8,128)S(1)}, u32[]{:S(2)}, u32[]{:S(2)}) collective-permute-start(f32[16,72,128]{2,1,0:T(8,128)S(1)} %get-tuple-element.23), channel_id=1, source_target_pairs={{0,8},{8,0},{1,9},{9,1},{2,10},{10,2},{3,11},{11,3},{4,12},{12,4},... | collective-permute-start | bytes 1769480 | tf_op jit(solution)/shard_map/ppermute | solution.py:363
  121.4 1.6 collective-permute-done.2
  123.1 21.3 %all_to_all.44.got_ref = f32[16,72,128]{2,1,0:T(8,128)S(1)} all-to-all(f32[16,72,128]{2,1,0:T(8,128)S(1)} %add.7), channel_id=1, replica_groups=mesh['x_lo'=2,'z'=8,'core'=2,'x_hi'=2,'y'=4] {'x_lo','z'}, dimensions={0} | all-to-all | bytes 1179648 | tf_op jit(solution)/shard_map/all_to_all | solution.py:364
  145.3 17.1 %all_to_all.45 = f32[16,64,128]{2,1,0:T(8,128)S(1)} all-to-all(f32[16,64,128]{2,1,0:T(8,128)S(1)} %get-tuple-element.25), channel_id=1, replica_groups=mesh['x_lo'=2,'z'=8,'core'=2,'x_hi'=2,'y'=4] {'x_lo','z'}, dimensions={0} | all-to-all | bytes 1048576 | tf_op jit(solution)/shard_map/all_to_all | solution.py:365
  162.4 3.6 %collective-permute-start.3 = (f32[1024,128]{1,0:T(8,128)S(1)}, f32[1024,128]{1,0:T(8,128)S(1)}, u32[]{:S(2)}, u32[]{:S(2)}) collective-permute-start(f32[1024,128]{1,0:T(8,128)S(1)} %bitcast.11), channel_id=1, source_target_pairs={{0,8},{8,0},{1,9},{9,1},{2,10},{10,2},{3,11},{11,3},{4,12},{12,4},... | collective-permute-start | bytes 1572872 | tf_op jit(solution)/shard_map/ppermute | solution.py:366
  166.0 1.5 collective-permute-done.3.other_ref
  167.5 1.3 last.1
  168.8 3.3 %all-to-all-start.7 = ((f32[8,8,128]{2,1,0:T(8,128)}), f32[8,8,128]{2,1,0:T(8,128)S(1)}, u32[]{:S(2)}, u32[]{:S(2)}) async-start(f32[8,8,128]{2,1,0:T(8,128)} %get-tuple-element.26), calls=%async_computation.7 | async-start | bytes 65536 | tf_op jit(solution)/shard_map/all_to_all | solution.py:411
  173.4 5.4 %all-to-all-done.7.got_ref = f32[8,8,128]{2,1,0:T(8,128)S(1)} async-done(((f32[8,8,128]{2,1,0:T(8,128)}), f32[8,8,128]{2,1,0:T(8,128)S(1)}, u32[]{:S(2)}, u32[]{:S(2)}) %all-to-all-start.7) | async-done | bytes 32800 | tf_op jit(solution)/shard_map/all_to_all | solution.py:411
  178.7 2.1 %boot_factors.1 = f32[2048,128]{1,0:T(8,128)} custom-call(f32[8,8,128]{2,1,0:T(8,128)S(1)} %all-to-all-done.7.got_ref, f32[2048,128]{1,0:T(8,128)S(1)} %get-tuple-element.27.raw_ref), custom_call_target="tpu_custom_call" | custom-call | tf_op jit(solution)/shard_map/boot_factors/pallas_call | solution.py:418
  (10 shorter events, 4.8 us)
Async XLA Ops:
  0.6 22.0 %copy-start = (f32[2048,8]{0,1:T(8,128)S(1)}, f32[2048,8]{0,1:T(8,128)}, u32[]{:S(2)}) copy-start(f32[2048,8]{0,1:T(8,128)} %param.8) | copy-start | bytes 196612
  0.6 22.0 %copy-start.1 = (f32[1024,8]{0,1:T(8,128)S(1)}, f32[1024,8]{0,1:T(8,128)}, u32[]{:S(2)}) copy-start(f32[1024,8]{0,1:T(8,128)} %param.7) | copy-start | bytes 98308
  7.4 15.2 %all-to-all-start = ((f32[8,8,1152]{2,1,0:T(8,128)}), f32[8,8,1152]{2,1,0:T(8,128)S(1)}, u32[]{:S(2)}, u32[]{:S(2)}) async-start(f32[8,8,1152]{2,1,0:T(8,128)} %get-tuple-element.15), calls=%async_computation | async-start | bytes 589824 | tf_op jit(solution)/shard_map/all_to_all | solution.py:344
  27.4 4.0 %collective-permute-start = (f32[16,72,128]{2,1,0:T(8,128)S(1)}, f32[16,72,128]{2,1,0:T(8,128)S(1)}, u32[]{:S(2)}, u32[]{:S(2)}) collective-permute-start(f32[16,72,128]{2,1,0:T(8,128)S(1)} %get-tuple-element.18), channel_id=1, source_target_pairs={{0,8},{8,0},{1,9},{9,1},{2,10},{10,2},{3,11},{11,3},{4,12},{12,4},... | collective-permute-start | bytes 1769480 | tf_op jit(solution)/shard_map/ppermute | solution.py:363
  75.2 5.1 %collective-permute-start.1 = (f32[1024,128]{1,0:T(8,128)S(1)}, f32[1024,128]{1,0:T(8,128)S(1)}, u32[]{:S(2)}, u32[]{:S(2)}) collective-permute-start(f32[1024,128]{1,0:T(8,128)S(1)} %bitcast.13), channel_id=1, source_target_pairs={{0,8},{8,0},{1,9},{9,1},{2,10},{10,2},{3,11},{11,3},{4,12},{12,4},... | collective-permute-start | bytes 1572872 | tf_op jit(solution)/shard_map/ppermute | solution.py:366
  118.4 4.6 %collective-permute-start.2 = (f32[16,72,128]{2,1,0:T(8,128)S(1)}, f32[16,72,128]{2,1,0:T(8,128)S(1)}, u32[]{:S(2)}, u32[]{:S(2)}) collective-permute-start(f32[16,72,128]{2,1,0:T(8,128)S(1)} %get-tuple-element.23), channel_id=1, source_target_pairs={{0,8},{8,0},{1,9},{9,1},{2,10},{10,2},{3,11},{11,3},{4,12},{12,4},... | collective-permute-start | bytes 1769480 | tf_op jit(solution)/shard_map/ppermute | solution.py:363
  162.4 5.1 %collective-permute-start.3 = (f32[1024,128]{1,0:T(8,128)S(1)}, f32[1024,128]{1,0:T(8,128)S(1)}, u32[]{:S(2)}, u32[]{:S(2)}) collective-permute-start(f32[1024,128]{1,0:T(8,128)S(1)} %bitcast.11), channel_id=1, source_target_pairs={{0,8},{8,0},{1,9},{9,1},{2,10},{10,2},{3,11},{11,3},{4,12},{12,4},... | collective-permute-start | bytes 1572872 | tf_op jit(solution)/shard_map/ppermute | solution.py:366
  168.8 9.9 %all-to-all-start.7 = ((f32[8,8,128]{2,1,0:T(8,128)}), f32[8,8,128]{2,1,0:T(8,128)S(1)}, u32[]{:S(2)}, u32[]{:S(2)}) async-start(f32[8,8,128]{2,1,0:T(8,128)} %get-tuple-element.26), calls=%async_computation.7 | async-start | bytes 65536 | tf_op jit(solution)/shard_map/all_to_all | solution.py:411

commit v4 on v3

--- a/solution.py
+++ b/solution.py
@@ -95,7 +95,7 @@
     return jnp.where(row == lane, wide, 0.0)
 
 
-def put_signs(ids_ref, bits_ref, wide_ref, tall_ref):
+def signs_kernel(ids_ref, bits_ref, wide_ref, tall_ref):
     reps, clusters = bits_ref.shape
     n, firms = wide_ref.shape
     table = 2.0 * bits_ref[...].astype(jnp.float32) - 1.0
@@ -146,14 +146,14 @@
 
 
 def first_kernel(
-    start_any, factor_any, ids_any, bits_any, res_any,
-    out_ref, wide_ref, tall_ref,
-    start_ref, factor_ref, ids_ref, bits_ref, res_ref, total_ref, sems,
+    start_any, factor_any, res_any,
+    out_ref,
+    start_ref, factor_ref, res_ref, total_ref, sems,
 ):
     copies, factors, width = out_ref.shape
     firms, days = res_ref.shape
     n = total_ref.shape[1]
-    pairs = [(start_any, start_ref), (factor_any, factor_ref), (ids_any, ids_ref), (bits_any, bits_ref)]
+    pairs = [(start_any, start_ref), (factor_any, factor_ref)]
     small = [pltpu.make_async_copy(a, b, sems.at[STEPS * PIECES + i]) for i, (a, b) in enumerate(pairs)]
     for copy in small:
         copy.start()
@@ -168,7 +168,6 @@
     mixed = corners(fast(stack(start, "hl"), stack(factor_ref[...], "hl"), NT), factors, factors)
     mixed = jnp.concatenate([mixed, jnp.zeros((factors, width - firms - factors), jnp.float32)], axis=1)
     out_ref[:, :, firms:] = jnp.broadcast_to(mixed[None], (copies, factors, width - firms))
-    put_signs(ids_ref, bits_ref, wide_ref, tall_ref)
     for t in range(STEPS):
         arrive(large, t)
         high, low = split(res_ref[tiles[t]])
@@ -267,11 +266,12 @@
         out_ref[t * rows // block : (t + 1) * rows // block, 0:block, :] = part.reshape(rows // block, block, n)
 
 
-def turn_kernel(got_ref, out_ref, inverse_ref):
+def turn_kernel(got_ref, out_ref, *inverse_ref):
     copies, rows, _ = out_ref.shape
     total = got_ref[...].sum(axis=0)
     inverse = inverse_blocks(total[rows:], total.shape[0] - rows)
-    inverse_ref[...] = inverse
+    for ref in inverse_ref:
+        ref[...] = inverse
     chunk = exact(total[0:rows], inverse, NT)
     out_ref[...] = jnp.broadcast_to(chunk[None], out_ref.shape)
 
@@ -321,26 +321,26 @@
 
     residuals = in_hbm(residuals)
     block_scratch = [pltpu.VMEM((firms, days), jnp.float32), pltpu.SemaphoreType.DMA((STEPS * PIECES,))]
-    first, signs_t, signs = pl.pallas_call(
+    first = pl.pallas_call(
         first_kernel,
-        in_specs=[pl.BlockSpec(memory_space=pl.ANY)] * 5,
-        out_shape=(
-            shape(day_ranks, factors, firms + n),
-            shape(n, firms),
-            shape(firms, n),
-        ),
+        in_specs=[pl.BlockSpec(memory_space=pl.ANY)] * 3,
+        out_shape=shape(day_ranks, factors, firms + n),
         scratch_shapes=[
             pltpu.VMEM((factors, days), jnp.float32),
             pltpu.VMEM((factors, days), jnp.float32),
-            pltpu.VMEM((1, firms), jnp.int32),
-            pltpu.VMEM((reps, clusters), jnp.int32),
             pltpu.VMEM((firms, days), jnp.float32),
             pltpu.VMEM((firms, n), jnp.float32),
-            pltpu.SemaphoreType.DMA((STEPS * PIECES + 4,)),
+            pltpu.SemaphoreType.DMA((STEPS * PIECES + 2,)),
         ],
         compiler_params=PARAMS,
         name="first",
-    )(in_hbm(start_t), in_hbm(factor_t), in_hbm(cluster_ids.reshape(1, firms)), in_hbm(sign_bits.T), residuals)
+    )(in_hbm(start_t), in_hbm(factor_t), residuals)
+    signs_t, signs = pl.pallas_call(
+        signs_kernel,
+        out_shape=(shape(n, firms), shape(firms, n)),
+        compiler_params=PARAMS,
+        name="signs",
+    )(cluster_ids.reshape(1, firms), sign_bits.T)
     first = lax.all_to_all(first, ("x_hi", "y"), 0, 0, tiled=True)
 
     day_scratch = [
@@ -351,19 +351,22 @@
     ]
     parts = (chips, chunk + factors, n)
 
-    def turn(got, rows):
+    def turn(got, rows, with_inverse):
+        out = shape(got.shape[0], rows, n)
         return pl.pallas_call(
             turn_kernel,
-            out_shape=(shape(got.shape[0], rows, n), shape(n, n)),
+            out_shape=(out, shape(n, n)) if with_inverse else out,
             compiler_params=PARAMS,
             name="turn",
         )(got)
 
-    def sum_firms(send, keep):
+    def scatter_firms(send, keep):
         pair = keep + lax.ppermute(send, "core", [(0, 1), (1, 0)])
-        mine, inverse = turn(lax.all_to_all(pair, ("x_lo", "z"), 0, 0, tiled=True), chunk)
+        return lax.all_to_all(pair, ("x_lo", "z"), 0, 0, tiled=True)
+
+    def gather_firms(mine):
         mine = lax.all_to_all(mine, ("x_lo", "z"), 0, 0, tiled=True).reshape(half, n)
-        return mine, lax.ppermute(mine, "core", [(0, 1), (1, 0)]), inverse
+        return mine, lax.ppermute(mine, "core", [(0, 1), (1, 0)])
 
     send, keep = pl.pallas_call(
         days_first_kernel,
@@ -373,7 +376,7 @@
         compiler_params=PARAMS,
         name="days_first",
     )(core, first, signs_t, loadings_t, factor_t, residuals)
-    mine, other, _ = sum_firms(send, keep)
+    mine, other = gather_firms(turn(scatter_firms(send, keep), chunk, False))
 
     by_day = pl.pallas_call(
         firms_kernel,
@@ -388,7 +391,7 @@
         compiler_params=PARAMS,
         name="firms",
     )(core, mine, other, signs, loadings_t, factor_t, residuals)
-    raw_loads, _ = turn(lax.all_to_all(by_day, ("x_hi", "y"), 0, 0, tiled=True), block)
+    raw_loads = turn(lax.all_to_all(by_day, ("x_hi", "y"), 0, 0, tiled=True), block, False)
     raw_loads = lax.all_to_all(raw_loads, ("x_hi", "y"), 0, 0, tiled=True).reshape(firms, n)
 
     send, keep = pl.pallas_call(
@@ -399,7 +402,8 @@
         compiler_params=PARAMS,
         name="days_later",
     )(core, raw_loads, signs_t, loadings_t, factor_t, residuals)
-    mine, other, inverse = sum_firms(send, keep)
+    mine, inverse = turn(scatter_firms(send, keep), chunk, True)
+    mine, other = gather_firms(mine)
 
     raw_factors, last = pl.pallas_call(
         last_kernel,
@@ -408,13 +412,14 @@
         compiler_params=PARAMS,
         name="last",
     )(core, mine, other)
-    last = lax.all_to_all(last, ("x_hi", "y"), 0, 0, tiled=True)
     boot_loadings = pl.pallas_call(
         functools.partial(loadings_kernel, scale=math.sqrt(total_firms)),
         out_shape=shape(firms, n),
         compiler_params=PARAMS,
         name="boot_loadings",
     )(raw_loads, inverse)
+    last, boot_loadings = lax.optimization_barrier((last, boot_loadings))
+    last = lax.all_to_all(last, ("x_hi", "y"), 0, 0, tiled=True)
     boot_factors = pl.pallas_call(
         functools.partial(factors_kernel, scale=math.sqrt(total_days)),
         out_shape=shape(days, n),

time: 181 us -> 179 us (0.989)
  blocking collectives: 108 us -> 117 us
  waiting for transfers between devices: 19.4 us -> 12.4 us
  starting transfers between devices: 23.3 us -> 20 us
    all_to_all x4 -> x5, blocking collectives: 80.9 us -> 90.1 us  [the longest x2 46.6 us: scatter_firms(): return lax.all_to_all(pair, ('x_lo', 'z'), 0, 0, tiled=True)]
    all_to_all x1 -> x0, waiting for transfers between devices: 5.36 us -> none  [on_device(): last = lax.all_to_all(last, ('x_hi', 'y'), 0, 0, tiled=True)]
    all_to_all x1 -> x0, starting transfers between devices: 3.34 us -> none  [on_device(): last = lax.all_to_all(last, ('x_hi', 'y'), 0, 0, tiled=True)]
  transfers between devices with their start and end apart: 6 -> 5, of which waited for: 6 -> 5; matrix products, arithmetic and copies ran while one was open for 0% -> 0% of each run, Pallas kernels for 1% -> 1%
where the time goes in v4:
time: 179 us
  blocking collectives  117 us (65%)
  Pallas kernels  28.6 us (16%)
  starting transfers between devices  20 us (11%)
  waiting for transfers between devices  12.4 us (7%)
    all_to_all x2, blocking collectives, scatter_firms(): return lax.all_to_all(pair, ('x_lo', 'z'), 0, 0, tiled=True)  46.6 us
    all_to_all x2, blocking collectives, gather_firms(): lax.all_to_all(mine, ('x_lo', 'z'), 0, 0, tiled=True).reshape(half, n)  34.2 us
    all_to_all x1, blocking collectives, on_device(): lax.all_to_all(by_day, ('x_hi', 'y'), 0, 0, tiled=True)  14.4 us
    all_to_all x1, blocking collectives, on_device(): lax.all_to_all(raw_loads, ('x_hi', 'y'), 0, 0, tiled=True).reshape(firms, n)  12.4 us
    all_to_all x1, blocking collectives, on_device(): last = lax.all_to_all(last, ('x_hi', 'y'), 0, 0, tiled=True)  9.34 us
    all_to_all x1, starting transfers between devices, on_device(): first = lax.all_to_all(first, ('x_hi', 'y'), 0, 0, tiled=True)  7.49 us
    all_to_all x1, waiting for transfers between devices, on_device(): first = lax.all_to_all(first, ('x_hi', 'y'), 0, 0, tiled=True)  7.27 us
    ppermute x2, starting transfers between devices, gather_firms(): return (mine, lax.ppermute(mine, 'core', [(0, 1), (1, 0)]))  7.19 us
  transfers between devices with their start and end apart: 5, of which 5 were waited for; matrix products, arithmetic and copies ran while one was open for 0% of the time, Pallas kernels for 1%

profile of v4, /device:TPU:1, one launch (start us, length us, event | category | flops | bytes accessed | tf_op | source)
XLA Modules:
  0.0 178.8 jit_solution(146200505253409524)
XLA Ops:
  0.7 6.7 %first.1 = f32[8,8,1152]{2,1,0:T(8,128)} custom-call(f32[8,2048]{1,0:T(8,128)} %bitcast.24, f32[8,2048]{1,0:T(8,128)} %bitcast.15, f32[1024,2048]{1,0:T(8,128)} %res_any.7), custom_call_target="tpu_custom_call" | custom-call | tf_op jit(solution)/shard_map/first/pallas_call | solution.py:324
  7.4 7.5 %all-to-all-start = ((f32[8,8,1152]{2,1,0:T(8,128)}), f32[8,8,1152]{2,1,0:T(8,128)S(1)}, u32[]{:S(2)}, u32[]{:S(2)}) async-start(f32[8,8,1152]{2,1,0:T(8,128)} %first.1), calls=%async_computation | async-start | bytes 589824 | tf_op jit(solution)/shard_map/all_to_all | solution.py:344
  15.3 7.3 %all-to-all-done.got_ref = f32[8,8,1152]{2,1,0:T(8,128)S(1)} async-done(((f32[8,8,1152]{2,1,0:T(8,128)}), f32[8,8,1152]{2,1,0:T(8,128)S(1)}, u32[]{:S(2)}, u32[]{:S(2)}) %all-to-all-start) | async-done | bytes 294944 | tf_op jit(solution)/shard_map/all_to_all | solution.py:344
  22.6 4.8 %days_first.1 = (f32[16,72,128]{2,1,0:T(8,128)S(1)}, f32[16,72,128]{2,1,0:T(8,128)S(1)}) custom-call(s32[1]{0:T(128)} %bitcast.core_ref, f32[8,8,1152]{2,1,0:T(8,128)S(1)} %all-to-all-done.got_ref, f32[128,1024]{1,0:T(8,128)S(1)} %get-tuple-element.14.signs_ref, f32[8,1024]{1,0:T(8,128)S(1)} %bitcast.19, f32[8,2048]{1,0:T(8,128)S(1)} %bitcast.16, ...), custom_call_target="tpu_custom_call" | custom-call | tf_op jit(solution)/shard_map/days_first/pallas_call | solution.py:371
  27.3 2.4 %collective-permute-start = (f32[16,72,128]{2,1,0:T(8,128)S(1)}, f32[16,72,128]{2,1,0:T(8,128)S(1)}, u32[]{:S(2)}, u32[]{:S(2)}) collective-permute-start(f32[16,72,128]{2,1,0:T(8,128)S(1)} %get-tuple-element.16), channel_id=1, source_target_pairs={{0,8},{8,0},{1,9},{9,1},{2,10},{10,2},{3,11},{11,3},{4,12},{12,4},... | collective-permute-start | bytes 1769480 | tf_op jit(solution)/shard_map/ppermute | solution.py:364
  29.7 1.6 collective-permute-done
  31.4 25.4 %all_to_all.40.got_ref = f32[16,72,128]{2,1,0:T(8,128)S(1)} all-to-all(f32[16,72,128]{2,1,0:T(8,128)S(1)} %add.6), channel_id=1, replica_groups=mesh['x_lo'=2,'z'=8,'core'=2,'x_hi'=2,'y'=4] {'x_lo','z'}, dimensions={0} | all-to-all | bytes 1179648 | tf_op jit(solution)/shard_map/all_to_all | solution.py:365
  56.8 0.9 turn.3
  57.7 17.1 %all_to_all.41 = f32[16,64,128]{2,1,0:T(8,128)S(1)} all-to-all(f32[16,64,128]{2,1,0:T(8,128)S(1)} %turn.3), channel_id=1, replica_groups=mesh['x_lo'=2,'z'=8,'core'=2,'x_hi'=2,'y'=4] {'x_lo','z'}, dimensions={0} | all-to-all | bytes 1048576 | tf_op jit(solution)/shard_map/all_to_all | solution.py:368
  74.8 3.6 %collective-permute-start.1 = (f32[1024,128]{1,0:T(8,128)S(1)}, f32[1024,128]{1,0:T(8,128)S(1)}, u32[]{:S(2)}, u32[]{:S(2)}) collective-permute-start(f32[1024,128]{1,0:T(8,128)S(1)} %bitcast.13), channel_id=1, source_target_pairs={{0,8},{8,0},{1,9},{9,1},{2,10},{10,2},{3,11},{11,3},{4,12},{12,4},... | collective-permute-start | bytes 1572872 | tf_op jit(solution)/shard_map/ppermute | solution.py:369
  78.4 1.5 collective-permute-done.1.other_ref
  79.9 5.3 %firms.1 = f32[8,136,128]{2,1,0:T(8,128)S(1)} custom-call(s32[1]{0:T(128)} %bitcast.core_ref, f32[1024,128]{1,0:T(8,128)S(1)} %bitcast.14, f32[1024,128]{1,0:T(8,128)S(1)} %collective-permute-done.1.other_ref, f32[1024,128]{1,0:T(8,128)S(1)} %get-tuple-element.17.signs_ref, f32[8,1024]{1,0:T(8,128)S(1)} %bitcast.20, f32[8,2048]{1,0:T(8,128)S(1)} %bitcast.17, ...), custom_call_target="tpu_custom_call" | custom-call | tf_op jit(solution)/shard_map/firms/pallas_call | solution.py:381
  85.2 14.4 %all_to_all.42.got_ref = f32[8,136,128]{2,1,0:T(8,128)S(1)} all-to-all(f32[8,136,128]{2,1,0:T(8,128)S(1)} %firms.1), channel_id=1, replica_groups=mesh['x_lo'=2,'z'=8,'core'=2,'x_hi'=2,'y'=4] {'x_hi','y'}, dimensions={0} | all-to-all | bytes 1114112 | tf_op jit(solution)/shard_map/all_to_all | solution.py:394
  100.6 12.4 %all_to_all.43 = f32[8,128,128]{2,1,0:T(8,128)S(1)} all-to-all(f32[8,128,128]{2,1,0:T(8,128)S(1)} %turn.4), channel_id=1, replica_groups=mesh['x_lo'=2,'z'=8,'core'=2,'x_hi'=2,'y'=4] {'x_hi','y'}, dimensions={0} | all-to-all | bytes 1048576 | tf_op jit(solution)/shard_map/all_to_all | solution.py:395
  113.0 4.6 %days_later.1 = (f32[16,72,128]{2,1,0:T(8,128)S(1)}, f32[16,72,128]{2,1,0:T(8,128)S(1)}) custom-call(s32[1]{0:T(128)} %bitcast.core_ref, f32[1024,128]{1,0:T(8,128)S(1)} %bitcast.9, f32[128,1024]{1,0:T(8,128)S(1)} %get-tuple-element.14.signs_ref, f32[8,1024]{1,0:T(8,128)S(1)} %bitcast.21, f32[8,2048]{1,0:T(8,128)S(1)} %bitcast.18, f32[1024,2048]{1,0:T(8,128)} %res_any.7), custom_call_target="tpu_custom_call" | custom-call | tf_op jit(solution)/shard_map/days_later/pallas_call | solution.py:397
  117.6 3.0 %collective-permute-start.2 = (f32[16,72,128]{2,1,0:T(8,128)S(1)}, f32[16,72,128]{2,1,0:T(8,128)S(1)}, u32[]{:S(2)}, u32[]{:S(2)}) collective-permute-start(f32[16,72,128]{2,1,0:T(8,128)S(1)} %get-tuple-element.19), channel_id=1, source_target_pairs={{0,8},{8,0},{1,9},{9,1},{2,10},{10,2},{3,11},{11,3},{4,12},{12,4},... | collective-permute-start | bytes 1769480 | tf_op jit(solution)/shard_map/ppermute | solution.py:364
  120.6 1.6 collective-permute-done.2
  122.3 21.2 %all_to_all.44.got_ref = f32[16,72,128]{2,1,0:T(8,128)S(1)} all-to-all(f32[16,72,128]{2,1,0:T(8,128)S(1)} %add.7), channel_id=1, replica_groups=mesh['x_lo'=2,'z'=8,'core'=2,'x_hi'=2,'y'=4] {'x_lo','z'}, dimensions={0} | all-to-all | bytes 1179648 | tf_op jit(solution)/shard_map/all_to_all | solution.py:365
  143.5 0.9 turn.5
  144.4 17.1 %all_to_all.45 = f32[16,64,128]{2,1,0:T(8,128)S(1)} all-to-all(f32[16,64,128]{2,1,0:T(8,128)S(1)} %get-tuple-element.20), channel_id=1, replica_groups=mesh['x_lo'=2,'z'=8,'core'=2,'x_hi'=2,'y'=4] {'x_lo','z'}, dimensions={0} | all-to-all | bytes 1048576 | tf_op jit(solution)/shard_map/all_to_all | solution.py:368
  161.5 3.6 %collective-permute-start.3 = (f32[1024,128]{1,0:T(8,128)S(1)}, f32[1024,128]{1,0:T(8,128)S(1)}, u32[]{:S(2)}, u32[]{:S(2)}) collective-permute-start(f32[1024,128]{1,0:T(8,128)S(1)} %bitcast.11), channel_id=1, source_target_pairs={{0,8},{8,0},{1,9},{9,1},{2,10},{10,2},{3,11},{11,3},{4,12},{12,4},... | collective-permute-start | bytes 1572872 | tf_op jit(solution)/shard_map/ppermute | solution.py:369
  165.1 1.2 boot_loadings.1
  167.3 9.3 %all_to_all.46.got_ref = f32[8,8,128]{2,1,0:T(8,128)S(1)} all-to-all(f32[8,8,128]{2,1,0:T(8,128)S(1)} %get-tuple-element.24), channel_id=1, replica_groups=mesh['x_lo'=2,'z'=8,'core'=2,'x_hi'=2,'y'=4] {'x_hi','y'}, dimensions={0} | all-to-all | bytes 65536 | tf_op jit(solution)/shard_map/all_to_all | solution.py:422
  176.7 2.1 %boot_factors.1 = f32[2048,128]{1,0:T(8,128)} custom-call(f32[8,8,128]{2,1,0:T(8,128)S(1)} %all_to_all.46.got_ref, f32[2048,128]{1,0:T(8,128)S(1)} %get-tuple-element.25.raw_ref), custom_call_target="tpu_custom_call" | custom-call | tf_op jit(solution)/shard_map/boot_factors/pallas_call | solution.py:423
  (14 shorter events, 2.5 us)
Async XLA Ops:
  0.6 21.9 %copy-start = (f32[2048,8]{0,1:T(8,128)S(1)}, f32[2048,8]{0,1:T(8,128)}, u32[]{:S(2)}) copy-start(f32[2048,8]{0,1:T(8,128)} %param.8) | copy-start | bytes 196612
  0.6 14.2 %copy-start.2 = (s32[512,16]{0,1:T(8,128)S(1)}, s32[512,16]{0,1:T(8,128)}, u32[]{:S(2)}) copy-start(s32[512,16]{0,1:T(8,128)} %param.11) | copy-start | bytes 98308
  0.7 14.2 %copy-start.3 = (s32[1024]{0:T(1024)S(1)}, s32[1024]{0:T(1024)}, u32[]{:S(2)}) copy-start(s32[1024]{0:T(1024)} %param.10) | copy-start | bytes 12292
  0.7 21.9 %copy-start.1 = (f32[1024,8]{0,1:T(8,128)S(1)}, f32[1024,8]{0,1:T(8,128)}, u32[]{:S(2)}) copy-start(f32[1024,8]{0,1:T(8,128)} %param.7) | copy-start | bytes 98308
  7.4 15.2 %all-to-all-start = ((f32[8,8,1152]{2,1,0:T(8,128)}), f32[8,8,1152]{2,1,0:T(8,128)S(1)}, u32[]{:S(2)}, u32[]{:S(2)}) async-start(f32[8,8,1152]{2,1,0:T(8,128)} %first.1), calls=%async_computation | async-start | bytes 589824 | tf_op jit(solution)/shard_map/all_to_all | solution.py:344
  27.3 4.0 %collective-permute-start = (f32[16,72,128]{2,1,0:T(8,128)S(1)}, f32[16,72,128]{2,1,0:T(8,128)S(1)}, u32[]{:S(2)}, u32[]{:S(2)}) collective-permute-start(f32[16,72,128]{2,1,0:T(8,128)S(1)} %get-tuple-element.16), channel_id=1, source_target_pairs={{0,8},{8,0},{1,9},{9,1},{2,10},{10,2},{3,11},{11,3},{4,12},{12,4},... | collective-permute-start | bytes 1769480 | tf_op jit(solution)/shard_map/ppermute | solution.py:364
  74.8 5.1 %collective-permute-start.1 = (f32[1024,128]{1,0:T(8,128)S(1)}, f32[1024,128]{1,0:T(8,128)S(1)}, u32[]{:S(2)}, u32[]{:S(2)}) collective-permute-start(f32[1024,128]{1,0:T(8,128)S(1)} %bitcast.13), channel_id=1, source_target_pairs={{0,8},{8,0},{1,9},{9,1},{2,10},{10,2},{3,11},{11,3},{4,12},{12,4},... | collective-permute-start | bytes 1572872 | tf_op jit(solution)/shard_map/ppermute | solution.py:369
  117.6 4.6 %collective-permute-start.2 = (f32[16,72,128]{2,1,0:T(8,128)S(1)}, f32[16,72,128]{2,1,0:T(8,128)S(1)}, u32[]{:S(2)}, u32[]{:S(2)}) collective-permute-start(f32[16,72,128]{2,1,0:T(8,128)S(1)} %get-tuple-element.19), channel_id=1, source_target_pairs={{0,8},{8,0},{1,9},{9,1},{2,10},{10,2},{3,11},{11,3},{4,12},{12,4},... | collective-permute-start | bytes 1769480 | tf_op jit(solution)/shard_map/ppermute | solution.py:364
  161.5 5.1 %collective-permute-start.3 = (f32[1024,128]{1,0:T(8,128)S(1)}, f32[1024,128]{1,0:T(8,128)S(1)}, u32[]{:S(2)}, u32[]{:S(2)}) collective-permute-start(f32[1024,128]{1,0:T(8,128)S(1)} %bitcast.11), channel_id=1, source_target_pairs={{0,8},{8,0},{1,9},{9,1},{2,10},{10,2},{3,11},{11,3},{4,12},{12,4},... | collective-permute-start | bytes 1572872 | tf_op jit(solution)/shard_map/ppermute | solution.py:369

commit v5 on v4

--- a/solution.py
+++ b/solution.py
@@ -56,14 +56,16 @@
     return jnp.concatenate([parts[p] for p in order], axis=0).astype(jnp.bfloat16)
 
 
-def rotated(x, inverse):
-    n = inverse.shape[0]
-    high, low = split(x)
+def turning(inverse):
     top, rest = split(inverse.T)
-    right = jnp.concatenate(
+    return jnp.concatenate(
         [jnp.concatenate([top, rest], axis=1), jnp.concatenate([top, jnp.zeros_like(rest)], axis=1)], axis=0
     )
-    both = fast(jnp.concatenate([high, low], axis=1), right, NN)
+
+
+def rotated(x, right):
+    n = x.shape[1]
+    both = fast(jnp.concatenate(split(x), axis=1), right, NN)
     return both[:, 0:n] + both[:, n:]
 
 
@@ -80,13 +82,13 @@
     row = lax.broadcasted_iota(jnp.int32, (factors, n), 0)
     lane = lax.broadcasted_iota(jnp.int32, (factors, n), 1)
     first = (lane // factors) * factors
-    rest = gram
     inverse = jnp.where(row == lane - first, 1.0, 0.0)
+    spread = [jnp.take_along_axis(gram, first + j, axis=1, mode="promise_in_bounds") for j in range(factors)]
     for j in range(factors):
-        column = jnp.take_along_axis(rest, first + j, axis=1, mode="promise_in_bounds")
-        pivot = column[j : j + 1]
-        ratio = jnp.where(row > j, column / pivot, 0.0)
-        rest = rest - ratio * rest[j : j + 1]
+        pivot = spread[j][j : j + 1]
+        ratio = jnp.where(row > j, spread[j] / pivot, 0.0)
+        for k in range(j + 1, factors):
+            spread[k] = spread[k] - ratio * spread[k][j : j + 1]
         inverse = inverse - ratio * inverse[j : j + 1]
         inverse = jnp.where(row == j, inverse / jnp.sqrt(pivot), inverse)
     wide = jnp.concatenate([inverse] * (n // factors), axis=0)
@@ -276,23 +278,32 @@
     out_ref[...] = jnp.broadcast_to(chunk[None], out_ref.shape)
 
 
-def last_kernel(core_ref, mine_ref, other_ref, raw_ref, out_ref):
-    half = mine_ref.shape[0]
+def last_kernel(mine_ref, other_ref, out_ref):
     mine, other = mine_ref[...], other_ref[...]
-    core = core_ref[0]
-    raw_ref[pl.ds(pl.multiple_of(core * half, half), half), :] = mine
-    raw_ref[pl.ds(pl.multiple_of((1 - core) * half, half), half), :] = other
     gram = compact(gram_of(*split3(mine), TN, 1) + gram_of(*split3(other), TN, 1), out_ref.shape[1])
     out_ref[...] = jnp.broadcast_to(gram[None], out_ref.shape)
 
 
 def loadings_kernel(raw_ref, inverse_ref, out_ref, *, scale):
-    out_ref[...] = rotated(raw_ref[...], scale * inverse_ref[...])
-
-
-def factors_kernel(got_ref, raw_ref, out_ref, *, scale):
+    out_ref[...] = rotated(raw_ref[...], turning(scale * inverse_ref[...]))
+
+
+def factors_kernel(core_ref, got_ref, mine_ref, other_ref, out_any, buffer_ref, sems, *, scale):
+    half = mine_ref.shape[0]
+    rows = half // 2
     gram = got_ref[...].sum(axis=0)
-    out_ref[...] = rotated(raw_ref[...], scale * inverse_blocks(gram, gram.shape[0]))
+    right = turning(scale * inverse_blocks(gram, gram.shape[0]))
+    core = core_ref[0]
+    copies = []
+    for t in range(4):
+        ref, side = (mine_ref, core) if t < 2 else (other_ref, 1 - core)
+        at = slice(t % 2 * rows, (t % 2 + 1) * rows)
+        buffer_ref[t] = rotated(ref[at, :], right)
+        to = pl.ds(pl.multiple_of(side * half + t % 2 * rows, rows), rows)
+        copies.append(pltpu.make_async_copy(buffer_ref.at[t], out_any.at[to, :], sems.at[t]))
+        copies[t].start()
+    for copy in copies:
+        copy.wait()
 
 
 def shape(*dims):
@@ -349,6 +360,7 @@
         pltpu.VMEM((4 * factors, days), jnp.bfloat16),
         *block_scratch,
     ]
+    any_space = pl.BlockSpec(memory_space=pl.ANY)
     parts = (chips, chunk + factors, n)
 
     def turn(got, rows, with_inverse):
@@ -405,13 +417,12 @@
     mine, inverse = turn(scatter_firms(send, keep), chunk, True)
     mine, other = gather_firms(mine)
 
-    raw_factors, last = pl.pallas_call(
+    last = pl.pallas_call(
         last_kernel,
-        in_specs=inputs(2),
-        out_shape=(shape(days, n), shape(day_ranks, factors, n)),
+        out_shape=shape(day_ranks, factors, n),
         compiler_params=PARAMS,
         name="last",
-    )(core, mine, other)
+    )(mine, other)
     boot_loadings = pl.pallas_call(
         functools.partial(loadings_kernel, scale=math.sqrt(total_firms)),
         out_shape=shape(firms, n),
@@ -422,10 +433,13 @@
     last = lax.all_to_all(last, ("x_hi", "y"), 0, 0, tiled=True)
     boot_factors = pl.pallas_call(
         functools.partial(factors_kernel, scale=math.sqrt(total_days)),
+        in_specs=inputs(3),
+        out_specs=any_space,
         out_shape=shape(days, n),
+        scratch_shapes=[pltpu.VMEM((4, days // 4, n), jnp.float32), pltpu.SemaphoreType.DMA((4,))],
         compiler_params=PARAMS,
         name="boot_factors",
-    )(last, raw_factors)
+    )(core, last, mine, other)
     return boot_loadings, boot_factors
 
 

time: 179 us -> 178 us (level)
  Pallas kernels: 28.6 us -> 26.5 us
where the time goes in v5:
time: 178 us; the launch traced here: 177 us
  blocking collectives  117 us (66%)
  Pallas kernels  26.5 us (15%)
  starting transfers between devices  20 us (11%)
  waiting for transfers between devices  12.4 us (7%)
    all_to_all x2, blocking collectives, scatter_firms(): return lax.all_to_all(pair, ('x_lo', 'z'), 0, 0, tiled=True)  46.6 us
    all_to_all x2, blocking collectives, gather_firms(): lax.all_to_all(mine, ('x_lo', 'z'), 0, 0, tiled=True).reshape(half, n)  34.2 us
    all_to_all x1, blocking collectives, on_device(): lax.all_to_all(by_day, ('x_hi', 'y'), 0, 0, tiled=True)  14.6 us
    all_to_all x1, blocking collectives, on_device(): lax.all_to_all(raw_loads, ('x_hi', 'y'), 0, 0, tiled=True).reshape(firms, n)  12.4 us
    all_to_all x1, blocking collectives, on_device(): last = lax.all_to_all(last, ('x_hi', 'y'), 0, 0, tiled=True)  9.34 us
    all_to_all x1, starting transfers between devices, on_device(): first = lax.all_to_all(first, ('x_hi', 'y'), 0, 0, tiled=True)  7.49 us
    all_to_all x1, waiting for transfers between devices, on_device(): first = lax.all_to_all(first, ('x_hi', 'y'), 0, 0, tiled=True)  7.27 us
    ppermute x2, starting transfers between devices, gather_firms(): return (mine, lax.ppermute(mine, 'core', [(0, 1), (1, 0)]))  7.19 us
  transfers between devices with their start and end apart: 5, of which 5 were waited for; matrix products, arithmetic and copies ran while one was open for 0% of the time, Pallas kernels for 1%

profile of v5, /device:TPU:1, one launch (start us, length us, event | category | flops | bytes accessed | tf_op | source)
XLA Modules:
  0.0 177.1 jit_solution(3917032185893276624)
XLA Ops:
  0.7 6.7 %first.1 = f32[8,8,1152]{2,1,0:T(8,128)} custom-call(f32[8,2048]{1,0:T(8,128)} %bitcast.25, f32[8,2048]{1,0:T(8,128)} %bitcast.16, f32[1024,2048]{1,0:T(8,128)} %res_any.7), custom_call_target="tpu_custom_call" | custom-call | tf_op jit(solution)/shard_map/first/pallas_call | solution.py:335
  7.4 7.5 %all-to-all-start = ((f32[8,8,1152]{2,1,0:T(8,128)}), f32[8,8,1152]{2,1,0:T(8,128)S(1)}, u32[]{:S(2)}, u32[]{:S(2)}) async-start(f32[8,8,1152]{2,1,0:T(8,128)} %first.1), calls=%async_computation | async-start | bytes 589824 | tf_op jit(solution)/shard_map/all_to_all | solution.py:355
  15.3 7.3 %all-to-all-done.got_ref = f32[8,8,1152]{2,1,0:T(8,128)S(1)} async-done(((f32[8,8,1152]{2,1,0:T(8,128)}), f32[8,8,1152]{2,1,0:T(8,128)S(1)}, u32[]{:S(2)}, u32[]{:S(2)}) %all-to-all-start) | async-done | bytes 294944 | tf_op jit(solution)/shard_map/all_to_all | solution.py:355
  22.6 4.8 %days_first.1 = (f32[16,72,128]{2,1,0:T(8,128)S(1)}, f32[16,72,128]{2,1,0:T(8,128)S(1)}) custom-call(s32[1]{0:T(128)} %bitcast.core_ref, f32[8,8,1152]{2,1,0:T(8,128)S(1)} %all-to-all-done.got_ref, f32[128,1024]{1,0:T(8,128)S(1)} %get-tuple-element.12.signs_ref, f32[8,1024]{1,0:T(8,128)S(1)} %bitcast.20, f32[8,2048]{1,0:T(8,128)S(1)} %bitcast.17, ...), custom_call_target="tpu_custom_call" | custom-call | tf_op jit(solution)/shard_map/days_first/pallas_call | solution.py:383
  27.3 2.4 %collective-permute-start = (f32[16,72,128]{2,1,0:T(8,128)S(1)}, f32[16,72,128]{2,1,0:T(8,128)S(1)}, u32[]{:S(2)}, u32[]{:S(2)}) collective-permute-start(f32[16,72,128]{2,1,0:T(8,128)S(1)} %get-tuple-element.14), channel_id=1, source_target_pairs={{0,8},{8,0},{1,9},{9,1},{2,10},{10,2},{3,11},{11,3},{4,12},{12,4},... | collective-permute-start | bytes 1769480 | tf_op jit(solution)/shard_map/ppermute | solution.py:376
  29.7 1.6 collective-permute-done
  31.4 25.4 %all_to_all.40.got_ref = f32[16,72,128]{2,1,0:T(8,128)S(1)} all-to-all(f32[16,72,128]{2,1,0:T(8,128)S(1)} %add.6), channel_id=1, replica_groups=mesh['x_lo'=2,'z'=8,'core'=2,'x_hi'=2,'y'=4] {'x_lo','z'}, dimensions={0} | all-to-all | bytes 1179648 | tf_op jit(solution)/shard_map/all_to_all | solution.py:377
  57.3 17.1 %all_to_all.41 = f32[16,64,128]{2,1,0:T(8,128)S(1)} all-to-all(f32[16,64,128]{2,1,0:T(8,128)S(1)} %turn.3), channel_id=1, replica_groups=mesh['x_lo'=2,'z'=8,'core'=2,'x_hi'=2,'y'=4] {'x_lo','z'}, dimensions={0} | all-to-all | bytes 1048576 | tf_op jit(solution)/shard_map/all_to_all | solution.py:380
  74.3 3.6 %collective-permute-start.1 = (f32[1024,128]{1,0:T(8,128)S(1)}, f32[1024,128]{1,0:T(8,128)S(1)}, u32[]{:S(2)}, u32[]{:S(2)}) collective-permute-start(f32[1024,128]{1,0:T(8,128)S(1)} %bitcast.14), channel_id=1, source_target_pairs={{0,8},{8,0},{1,9},{9,1},{2,10},{10,2},{3,11},{11,3},{4,12},{12,4},... | collective-permute-start | bytes 1572872 | tf_op jit(solution)/shard_map/ppermute | solution.py:381
  77.9 1.5 collective-permute-done.1.other_ref
  79.5 5.3 %firms.1 = f32[8,136,128]{2,1,0:T(8,128)S(1)} custom-call(s32[1]{0:T(128)} %bitcast.core_ref, f32[1024,128]{1,0:T(8,128)S(1)} %bitcast.15, f32[1024,128]{1,0:T(8,128)S(1)} %collective-permute-done.1.other_ref, f32[1024,128]{1,0:T(8,128)S(1)} %get-tuple-element.15.signs_ref, f32[8,1024]{1,0:T(8,128)S(1)} %bitcast.21, f32[8,2048]{1,0:T(8,128)S(1)} %bitcast.18, ...), custom_call_target="tpu_custom_call" | custom-call | tf_op jit(solution)/shard_map/firms/pallas_call | solution.py:393
  84.8 14.6 %all_to_all.42.got_ref = f32[8,136,128]{2,1,0:T(8,128)S(1)} all-to-all(f32[8,136,128]{2,1,0:T(8,128)S(1)} %firms.1), channel_id=1, replica_groups=mesh['x_lo'=2,'z'=8,'core'=2,'x_hi'=2,'y'=4] {'x_hi','y'}, dimensions={0} | all-to-all | bytes 1114112 | tf_op jit(solution)/shard_map/all_to_all | solution.py:406
  99.8 12.4 %all_to_all.43 = f32[8,128,128]{2,1,0:T(8,128)S(1)} all-to-all(f32[8,128,128]{2,1,0:T(8,128)S(1)} %turn.4), channel_id=1, replica_groups=mesh['x_lo'=2,'z'=8,'core'=2,'x_hi'=2,'y'=4] {'x_hi','y'}, dimensions={0} | all-to-all | bytes 1048576 | tf_op jit(solution)/shard_map/all_to_all | solution.py:407
  112.2 4.7 %days_later.1 = (f32[16,72,128]{2,1,0:T(8,128)S(1)}, f32[16,72,128]{2,1,0:T(8,128)S(1)}) custom-call(s32[1]{0:T(128)} %bitcast.core_ref, f32[1024,128]{1,0:T(8,128)S(1)} %bitcast.9, f32[128,1024]{1,0:T(8,128)S(1)} %get-tuple-element.12.signs_ref, f32[8,1024]{1,0:T(8,128)S(1)} %bitcast.22, f32[8,2048]{1,0:T(8,128)S(1)} %bitcast.19, f32[1024,2048]{1,0:T(8,128)} %res_any.7), custom_call_target="tpu_custom_call" | custom-call | tf_op jit(solution)/shard_map/days_later/pallas_call | solution.py:409
  116.9 3.0 %collective-permute-start.2 = (f32[16,72,128]{2,1,0:T(8,128)S(1)}, f32[16,72,128]{2,1,0:T(8,128)S(1)}, u32[]{:S(2)}, u32[]{:S(2)}) collective-permute-start(f32[16,72,128]{2,1,0:T(8,128)S(1)} %get-tuple-element.17), channel_id=1, source_target_pairs={{0,8},{8,0},{1,9},{9,1},{2,10},{10,2},{3,11},{11,3},{4,12},{12,4},... | collective-permute-start | bytes 1769480 | tf_op jit(solution)/shard_map/ppermute | solution.py:376
  119.8 1.6 collective-permute-done.2
  121.5 21.2 %all_to_all.44.got_ref = f32[16,72,128]{2,1,0:T(8,128)S(1)} all-to-all(f32[16,72,128]{2,1,0:T(8,128)S(1)} %add.7), channel_id=1, replica_groups=mesh['x_lo'=2,'z'=8,'core'=2,'x_hi'=2,'y'=4] {'x_lo','z'}, dimensions={0} | all-to-all | bytes 1179648 | tf_op jit(solution)/shard_map/all_to_all | solution.py:377
  142.7 0.4 turn.5
  143.2 17.1 %all_to_all.45 = f32[16,64,128]{2,1,0:T(8,128)S(1)} all-to-all(f32[16,64,128]{2,1,0:T(8,128)S(1)} %get-tuple-element.18), channel_id=1, replica_groups=mesh['x_lo'=2,'z'=8,'core'=2,'x_hi'=2,'y'=4] {'x_lo','z'}, dimensions={0} | all-to-all | bytes 1048576 | tf_op jit(solution)/shard_map/all_to_all | solution.py:380
  160.3 3.6 %collective-permute-start.3 = (f32[1024,128]{1,0:T(8,128)S(1)}, f32[1024,128]{1,0:T(8,128)S(1)}, u32[]{:S(2)}, u32[]{:S(2)}) collective-permute-start(f32[1024,128]{1,0:T(8,128)S(1)} %bitcast.11), channel_id=1, source_target_pairs={{0,8},{8,0},{1,9},{9,1},{2,10},{10,2},{3,11},{11,3},{4,12},{12,4},... | collective-permute-start | bytes 1572872 | tf_op jit(solution)/shard_map/ppermute | solution.py:381
  163.9 1.2 boot_loadings.1
  165.4 0.6 last.1
  166.0 9.3 %all_to_all.46.got_ref = f32[8,8,128]{2,1,0:T(8,128)S(1)} all-to-all(f32[8,8,128]{2,1,0:T(8,128)S(1)} %last.1), channel_id=1, replica_groups=mesh['x_lo'=2,'z'=8,'core'=2,'x_hi'=2,'y'=4] {'x_hi','y'}, dimensions={0} | all-to-all | bytes 65536 | tf_op jit(solution)/shard_map/all_to_all | solution.py:433
  175.4 1.6 boot_factors.1
  (14 shorter events, 1.8 us)
Async XLA Ops:
  0.6 21.9 %copy-start = (f32[2048,8]{0,1:T(8,128)S(1)}, f32[2048,8]{0,1:T(8,128)}, u32[]{:S(2)}) copy-start(f32[2048,8]{0,1:T(8,128)} %param.8) | copy-start | bytes 196612
  0.6 14.2 %copy-start.2 = (s32[512,16]{0,1:T(8,128)S(1)}, s32[512,16]{0,1:T(8,128)}, u32[]{:S(2)}) copy-start(s32[512,16]{0,1:T(8,128)} %param.11) | copy-start | bytes 98308
  0.7 14.2 %copy-start.3 = (s32[1024]{0:T(1024)S(1)}, s32[1024]{0:T(1024)}, u32[]{:S(2)}) copy-start(s32[1024]{0:T(1024)} %param.10) | copy-start | bytes 12292
  0.7 21.9 %copy-start.1 = (f32[1024,8]{0,1:T(8,128)S(1)}, f32[1024,8]{0,1:T(8,128)}, u32[]{:S(2)}) copy-start(f32[1024,8]{0,1:T(8,128)} %param.7) | copy-start | bytes 98308
  7.4 15.2 %all-to-all-start = ((f32[8,8,1152]{2,1,0:T(8,128)}), f32[8,8,1152]{2,1,0:T(8,128)S(1)}, u32[]{:S(2)}, u32[]{:S(2)}) async-start(f32[8,8,1152]{2,1,0:T(8,128)} %first.1), calls=%async_computation | async-start | bytes 589824 | tf_op jit(solution)/shard_map/all_to_all | solution.py:355
  27.3 4.0 %collective-permute-start = (f32[16,72,128]{2,1,0:T(8,128)S(1)}, f32[16,72,128]{2,1,0:T(8,128)S(1)}, u32[]{:S(2)}, u32[]{:S(2)}) collective-permute-start(f32[16,72,128]{2,1,0:T(8,128)S(1)} %get-tuple-element.14), channel_id=1, source_target_pairs={{0,8},{8,0},{1,9},{9,1},{2,10},{10,2},{3,11},{11,3},{4,12},{12,4},... | collective-permute-start | bytes 1769480 | tf_op jit(solution)/shard_map/ppermute | solution.py:376
  74.3 5.1 %collective-permute-start.1 = (f32[1024,128]{1,0:T(8,128)S(1)}, f32[1024,128]{1,0:T(8,128)S(1)}, u32[]{:S(2)}, u32[]{:S(2)}) collective-permute-start(f32[1024,128]{1,0:T(8,128)S(1)} %bitcast.14), channel_id=1, source_target_pairs={{0,8},{8,0},{1,9},{9,1},{2,10},{10,2},{3,11},{11,3},{4,12},{12,4},... | collective-permute-start | bytes 1572872 | tf_op jit(solution)/shard_map/ppermute | solution.py:381
  116.9 4.6 %collective-permute-start.2 = (f32[16,72,128]{2,1,0:T(8,128)S(1)}, f32[16,72,128]{2,1,0:T(8,128)S(1)}, u32[]{:S(2)}, u32[]{:S(2)}) collective-permute-start(f32[16,72,128]{2,1,0:T(8,128)S(1)} %get-tuple-element.17), channel_id=1, source_target_pairs={{0,8},{8,0},{1,9},{9,1},{2,10},{10,2},{3,11},{11,3},{4,12},{12,4},... | collective-permute-start | bytes 1769480 | tf_op jit(solution)/shard_map/ppermute | solution.py:376
  160.3 5.1 %collective-permute-start.3 = (f32[1024,128]{1,0:T(8,128)S(1)}, f32[1024,128]{1,0:T(8,128)S(1)}, u32[]{:S(2)}, u32[]{:S(2)}) collective-permute-start(f32[1024,128]{1,0:T(8,128)S(1)} %bitcast.11), channel_id=1, source_target_pairs={{0,8},{8,0},{1,9},{9,1},{2,10},{10,2},{3,11},{11,3},{4,12},{12,4},... | collective-permute-start | bytes 1572872 | tf_op jit(solution)/shard_map/ppermute | solution.py:381

commit v6 on v5

--- a/solution.py
+++ b/solution.py
@@ -240,19 +240,20 @@
     days_tiles(copies, firsts, res_ref, left_ref, small_ref, right_ref, send_ref, keep_ref)
 
 
-def firms_kernel(core_ref, mine_ref, other_ref, signs_ref, loadings_ref, factor_ref, res_any, out_ref, raw_ref, right_ref, add_ref, res_ref, sems):
+def firms_kernel(core_ref, mine_ref, other_ref, signs_ref, loadings_ref, factor_ref, res_any, out_ref, right_ref, add_ref, res_ref, sems):
     factors = loadings_ref.shape[0]
     half, n = mine_ref.shape
     rows = res_ref.shape[0] // STEPS
     large = bring(piece_pairs(res_any, res_ref, rows_of), sems)
     core = core_ref[0]
-    raw_ref[pl.ds(pl.multiple_of(core * half, half), half), :] = mine_ref[...]
-    raw_ref[pl.ds(pl.multiple_of((1 - core) * half, half), half), :] = other_ref[...]
-    raw = raw_ref[...]
-    high, middle, low = split3(raw)
-    right_ref[:, 0:n] = high
-    right_ref[:, n:] = middle
-    gram = compact(gram_of(high, middle, low, TN, 1), factors)
+    gram = jnp.zeros((n, n), jnp.float32)
+    for ref, side in ((mine_ref, core), (other_ref, 1 - core)):
+        high, middle, low = split3(ref[...])
+        at = pl.ds(pl.multiple_of(side * half, half), half)
+        right_ref[at, 0:n] = high
+        right_ref[at, n:] = middle
+        gram = gram + gram_of(high, middle, low, TN, 1)
+    gram = compact(gram, factors)
     copies, total = out_ref.shape[0], out_ref.shape[1]
     out_ref[:, total - factors :, :] = jnp.broadcast_to(gram[None], (copies, factors, n))
     small = corners(fast(stack(factor_ref[...], "hl"), right_ref[...], NN), factors, n)
@@ -394,7 +395,6 @@
         firms_kernel,
         in_specs=inputs(5) + [pl.BlockSpec(memory_space=pl.ANY)],
         scratch_shapes=[
-            pltpu.VMEM((days, n), jnp.float32),
             pltpu.VMEM((days, 2 * n), jnp.bfloat16),
             pltpu.VMEM((firms, n), jnp.float32),
             *block_scratch,

time: 178 us -> 177 us (level)
  no operation moved by 1% of the time
where the time goes in v6:
time: 177 us
  blocking collectives  117 us (66%)
  Pallas kernels  26 us (15%)
  starting transfers between devices  20 us (11%)
  waiting for transfers between devices  12.4 us (7%)
    all_to_all x2, blocking collectives, scatter_firms(): return lax.all_to_all(pair, ('x_lo', 'z'), 0, 0, tiled=True)  46.5 us
    all_to_all x2, blocking collectives, gather_firms(): lax.all_to_all(mine, ('x_lo', 'z'), 0, 0, tiled=True).reshape(half, n)  34.2 us
    all_to_all x1, blocking collectives, on_device(): lax.all_to_all(by_day, ('x_hi', 'y'), 0, 0, tiled=True)  14.6 us
    all_to_all x1, blocking collectives, on_device(): lax.all_to_all(raw_loads, ('x_hi', 'y'), 0, 0, tiled=True).reshape(firms, n)  12.4 us
    all_to_all x1, blocking collectives, on_device(): last = lax.all_to_all(last, ('x_hi', 'y'), 0, 0, tiled=True)  9.36 us
    all_to_all x1, starting transfers between devices, on_device(): first = lax.all_to_all(first, ('x_hi', 'y'), 0, 0, tiled=True)  7.49 us
    all_to_all x1, waiting for transfers between devices, on_device(): first = lax.all_to_all(first, ('x_hi', 'y'), 0, 0, tiled=True)  7.27 us
    ppermute x2, starting transfers between devices, gather_firms(): return (mine, lax.ppermute(mine, 'core', [(0, 1), (1, 0)]))  7.19 us
  transfers between devices with their start and end apart: 5, of which 5 were waited for; matrix products, arithmetic and copies ran while one was open for 0% of the time, Pallas kernels for 1%

profile of v6, /device:TPU:1, one launch (start us, length us, event | category | flops | bytes accessed | tf_op | source)
XLA Modules:
  0.0 176.5 jit_solution(8604628608151957366)
XLA Ops:
  0.7 6.7 %first.1 = f32[8,8,1152]{2,1,0:T(8,128)} custom-call(f32[8,2048]{1,0:T(8,128)} %bitcast.25, f32[8,2048]{1,0:T(8,128)} %bitcast.16, f32[1024,2048]{1,0:T(8,128)} %res_any.7), custom_call_target="tpu_custom_call" | custom-call | tf_op jit(solution)/shard_map/first/pallas_call | solution.py:336
  7.4 7.5 %all-to-all-start = ((f32[8,8,1152]{2,1,0:T(8,128)}), f32[8,8,1152]{2,1,0:T(8,128)S(1)}, u32[]{:S(2)}, u32[]{:S(2)}) async-start(f32[8,8,1152]{2,1,0:T(8,128)} %first.1), calls=%async_computation | async-start | bytes 589824 | tf_op jit(solution)/shard_map/all_to_all | solution.py:356
  15.3 7.3 %all-to-all-done.got_ref = f32[8,8,1152]{2,1,0:T(8,128)S(1)} async-done(((f32[8,8,1152]{2,1,0:T(8,128)}), f32[8,8,1152]{2,1,0:T(8,128)S(1)}, u32[]{:S(2)}, u32[]{:S(2)}) %all-to-all-start) | async-done | bytes 294944 | tf_op jit(solution)/shard_map/all_to_all | solution.py:356
  22.6 4.8 %days_first.1 = (f32[16,72,128]{2,1,0:T(8,128)S(1)}, f32[16,72,128]{2,1,0:T(8,128)S(1)}) custom-call(s32[1]{0:T(128)} %bitcast.core_ref, f32[8,8,1152]{2,1,0:T(8,128)S(1)} %all-to-all-done.got_ref, f32[128,1024]{1,0:T(8,128)S(1)} %get-tuple-element.12.signs_ref, f32[8,1024]{1,0:T(8,128)S(1)} %bitcast.20, f32[8,2048]{1,0:T(8,128)S(1)} %bitcast.17, ...), custom_call_target="tpu_custom_call" | custom-call | tf_op jit(solution)/shard_map/days_first/pallas_call | solution.py:384
  27.3 2.4 %collective-permute-start = (f32[16,72,128]{2,1,0:T(8,128)S(1)}, f32[16,72,128]{2,1,0:T(8,128)S(1)}, u32[]{:S(2)}, u32[]{:S(2)}) collective-permute-start(f32[16,72,128]{2,1,0:T(8,128)S(1)} %get-tuple-element.14), channel_id=1, source_target_pairs={{0,8},{8,0},{1,9},{9,1},{2,10},{10,2},{3,11},{11,3},{4,12},{12,4},... | collective-permute-start | bytes 1769480 | tf_op jit(solution)/shard_map/ppermute | solution.py:377
  29.7 1.6 collective-permute-done
  31.4 25.4 %all_to_all.40.got_ref = f32[16,72,128]{2,1,0:T(8,128)S(1)} all-to-all(f32[16,72,128]{2,1,0:T(8,128)S(1)} %add.6), channel_id=1, replica_groups=mesh['x_lo'=2,'z'=8,'core'=2,'x_hi'=2,'y'=4] {'x_lo','z'}, dimensions={0} | all-to-all | bytes 1179648 | tf_op jit(solution)/shard_map/all_to_all | solution.py:378
  57.3 17.1 %all_to_all.41 = f32[16,64,128]{2,1,0:T(8,128)S(1)} all-to-all(f32[16,64,128]{2,1,0:T(8,128)S(1)} %turn.3), channel_id=1, replica_groups=mesh['x_lo'=2,'z'=8,'core'=2,'x_hi'=2,'y'=4] {'x_lo','z'}, dimensions={0} | all-to-all | bytes 1048576 | tf_op jit(solution)/shard_map/all_to_all | solution.py:381
  74.3 3.6 %collective-permute-start.1 = (f32[1024,128]{1,0:T(8,128)S(1)}, f32[1024,128]{1,0:T(8,128)S(1)}, u32[]{:S(2)}, u32[]{:S(2)}) collective-permute-start(f32[1024,128]{1,0:T(8,128)S(1)} %bitcast.14), channel_id=1, source_target_pairs={{0,8},{8,0},{1,9},{9,1},{2,10},{10,2},{3,11},{11,3},{4,12},{12,4},... | collective-permute-start | bytes 1572872 | tf_op jit(solution)/shard_map/ppermute | solution.py:382
  77.9 1.5 collective-permute-done.1.other_ref
  79.5 4.7 %firms.1 = f32[8,136,128]{2,1,0:T(8,128)S(1)} custom-call(s32[1]{0:T(128)} %bitcast.core_ref, f32[1024,128]{1,0:T(8,128)S(1)} %bitcast.15, f32[1024,128]{1,0:T(8,128)S(1)} %collective-permute-done.1.other_ref, f32[1024,128]{1,0:T(8,128)S(1)} %get-tuple-element.15.signs_ref, f32[8,1024]{1,0:T(8,128)S(1)} %bitcast.21, f32[8,2048]{1,0:T(8,128)S(1)} %bitcast.18, ...), custom_call_target="tpu_custom_call" | custom-call | tf_op jit(solution)/shard_map/firms/pallas_call | solution.py:394
  84.2 14.6 %all_to_all.42.got_ref = f32[8,136,128]{2,1,0:T(8,128)S(1)} all-to-all(f32[8,136,128]{2,1,0:T(8,128)S(1)} %firms.1), channel_id=1, replica_groups=mesh['x_lo'=2,'z'=8,'core'=2,'x_hi'=2,'y'=4] {'x_hi','y'}, dimensions={0} | all-to-all | bytes 1114112 | tf_op jit(solution)/shard_map/all_to_all | solution.py:406
  99.3 12.4 %all_to_all.43 = f32[8,128,128]{2,1,0:T(8,128)S(1)} all-to-all(f32[8,128,128]{2,1,0:T(8,128)S(1)} %turn.4), channel_id=1, replica_groups=mesh['x_lo'=2,'z'=8,'core'=2,'x_hi'=2,'y'=4] {'x_hi','y'}, dimensions={0} | all-to-all | bytes 1048576 | tf_op jit(solution)/shard_map/all_to_all | solution.py:407
  111.6 4.7 %days_later.1 = (f32[16,72,128]{2,1,0:T(8,128)S(1)}, f32[16,72,128]{2,1,0:T(8,128)S(1)}) custom-call(s32[1]{0:T(128)} %bitcast.core_ref, f32[1024,128]{1,0:T(8,128)S(1)} %bitcast.9, f32[128,1024]{1,0:T(8,128)S(1)} %get-tuple-element.12.signs_ref, f32[8,1024]{1,0:T(8,128)S(1)} %bitcast.22, f32[8,2048]{1,0:T(8,128)S(1)} %bitcast.19, f32[1024,2048]{1,0:T(8,128)} %res_any.7), custom_call_target="tpu_custom_call" | custom-call | tf_op jit(solution)/shard_map/days_later/pallas_call | solution.py:409
  116.3 2.9 %collective-permute-start.2 = (f32[16,72,128]{2,1,0:T(8,128)S(1)}, f32[16,72,128]{2,1,0:T(8,128)S(1)}, u32[]{:S(2)}, u32[]{:S(2)}) collective-permute-start(f32[16,72,128]{2,1,0:T(8,128)S(1)} %get-tuple-element.17), channel_id=1, source_target_pairs={{0,8},{8,0},{1,9},{9,1},{2,10},{10,2},{3,11},{11,3},{4,12},{12,4},... | collective-permute-start | bytes 1769480 | tf_op jit(solution)/shard_map/ppermute | solution.py:377
  119.3 1.6 collective-permute-done.2
  121.0 21.1 %all_to_all.44.got_ref = f32[16,72,128]{2,1,0:T(8,128)S(1)} all-to-all(f32[16,72,128]{2,1,0:T(8,128)S(1)} %add.7), channel_id=1, replica_groups=mesh['x_lo'=2,'z'=8,'core'=2,'x_hi'=2,'y'=4] {'x_lo','z'}, dimensions={0} | all-to-all | bytes 1179648 | tf_op jit(solution)/shard_map/all_to_all | solution.py:378
  142.1 0.4 turn.5
  142.6 17.1 %all_to_all.45 = f32[16,64,128]{2,1,0:T(8,128)S(1)} all-to-all(f32[16,64,128]{2,1,0:T(8,128)S(1)} %get-tuple-element.18), channel_id=1, replica_groups=mesh['x_lo'=2,'z'=8,'core'=2,'x_hi'=2,'y'=4] {'x_lo','z'}, dimensions={0} | all-to-all | bytes 1048576 | tf_op jit(solution)/shard_map/all_to_all | solution.py:381
  159.6 3.6 %collective-permute-start.3 = (f32[1024,128]{1,0:T(8,128)S(1)}, f32[1024,128]{1,0:T(8,128)S(1)}, u32[]{:S(2)}, u32[]{:S(2)}) collective-permute-start(f32[1024,128]{1,0:T(8,128)S(1)} %bitcast.11), channel_id=1, source_target_pairs={{0,8},{8,0},{1,9},{9,1},{2,10},{10,2},{3,11},{11,3},{4,12},{12,4},... | collective-permute-start | bytes 1572872 | tf_op jit(solution)/shard_map/ppermute | solution.py:382
  163.2 1.2 boot_loadings.1
  164.8 0.6 last.1
  165.4 9.4 %all_to_all.46.got_ref = f32[8,8,128]{2,1,0:T(8,128)S(1)} all-to-all(f32[8,8,128]{2,1,0:T(8,128)S(1)} %last.1), channel_id=1, replica_groups=mesh['x_lo'=2,'z'=8,'core'=2,'x_hi'=2,'y'=4] {'x_hi','y'}, dimensions={0} | all-to-all | bytes 65536 | tf_op jit(solution)/shard_map/all_to_all | solution.py:433
  174.8 1.6 boot_factors.1
  (14 shorter events, 1.8 us)
Async XLA Ops:
  0.6 21.9 %copy-start = (f32[2048,8]{0,1:T(8,128)S(1)}, f32[2048,8]{0,1:T(8,128)}, u32[]{:S(2)}) copy-start(f32[2048,8]{0,1:T(8,128)} %param.8) | copy-start | bytes 196612
  0.6 14.2 %copy-start.2 = (s32[512,16]{0,1:T(8,128)S(1)}, s32[512,16]{0,1:T(8,128)}, u32[]{:S(2)}) copy-start(s32[512,16]{0,1:T(8,128)} %param.11) | copy-start | bytes 98308
  0.7 14.2 %copy-start.3 = (s32[1024]{0:T(1024)S(1)}, s32[1024]{0:T(1024)}, u32[]{:S(2)}) copy-start(s32[1024]{0:T(1024)} %param.10) | copy-start | bytes 12292
  0.7 21.9 %copy-start.1 = (f32[1024,8]{0,1:T(8,128)S(1)}, f32[1024,8]{0,1:T(8,128)}, u32[]{:S(2)}) copy-start(f32[1024,8]{0,1:T(8,128)} %param.7) | copy-start | bytes 98308
  7.4 15.2 %all-to-all-start = ((f32[8,8,1152]{2,1,0:T(8,128)}), f32[8,8,1152]{2,1,0:T(8,128)S(1)}, u32[]{:S(2)}, u32[]{:S(2)}) async-start(f32[8,8,1152]{2,1,0:T(8,128)} %first.1), calls=%async_computation | async-start | bytes 589824 | tf_op jit(solution)/shard_map/all_to_all | solution.py:356
  27.3 4.0 %collective-permute-start = (f32[16,72,128]{2,1,0:T(8,128)S(1)}, f32[16,72,128]{2,1,0:T(8,128)S(1)}, u32[]{:S(2)}, u32[]{:S(2)}) collective-permute-start(f32[16,72,128]{2,1,0:T(8,128)S(1)} %get-tuple-element.14), channel_id=1, source_target_pairs={{0,8},{8,0},{1,9},{9,1},{2,10},{10,2},{3,11},{11,3},{4,12},{12,4},... | collective-permute-start | bytes 1769480 | tf_op jit(solution)/shard_map/ppermute | solution.py:377
  74.3 5.1 %collective-permute-start.1 = (f32[1024,128]{1,0:T(8,128)S(1)}, f32[1024,128]{1,0:T(8,128)S(1)}, u32[]{:S(2)}, u32[]{:S(2)}) collective-permute-start(f32[1024,128]{1,0:T(8,128)S(1)} %bitcast.14), channel_id=1, source_target_pairs={{0,8},{8,0},{1,9},{9,1},{2,10},{10,2},{3,11},{11,3},{4,12},{12,4},... | collective-permute-start | bytes 1572872 | tf_op jit(solution)/shard_map/ppermute | solution.py:382
  116.3 4.6 %collective-permute-start.2 = (f32[16,72,128]{2,1,0:T(8,128)S(1)}, f32[16,72,128]{2,1,0:T(8,128)S(1)}, u32[]{:S(2)}, u32[]{:S(2)}) collective-permute-start(f32[16,72,128]{2,1,0:T(8,128)S(1)} %get-tuple-element.17), channel_id=1, source_target_pairs={{0,8},{8,0},{1,9},{9,1},{2,10},{10,2},{3,11},{11,3},{4,12},{12,4},... | collective-permute-start | bytes 1769480 | tf_op jit(solution)/shard_map/ppermute | solution.py:377
  159.6 5.1 %collective-permute-start.3 = (f32[1024,128]{1,0:T(8,128)S(1)}, f32[1024,128]{1,0:T(8,128)S(1)}, u32[]{:S(2)}, u32[]{:S(2)}) collective-permute-start(f32[1024,128]{1,0:T(8,128)S(1)} %bitcast.11), channel_id=1, source_target_pairs={{0,8},{8,0},{1,9},{9,1},{2,10},{10,2},{3,11},{11,3},{4,12},{12,4},... | collective-permute-start | bytes 1572872 | tf_op jit(solution)/shard_map/ppermute | solution.py:382
